TPU v7x, 256 devices: a whole 4x4x8 slice. The times are simulated.
256 devices in a mesh: rep: 32 (over z_hi, y, x), inner: 8 (over z_lo, core).
Axes of the slice: x: 4, y: 4, z: 8 (z_hi: 2, z_lo: 4; z = z_hi * 4 + z_lo), core: 2. Of those that a mesh axis runs over, the one named last changes fastest.
Arguments:
- deltas: bfloat16 [32, 5120, 2560], P('rep', 'inner'), may hold values from -6 to 6
- master_weight: float32 [5120, 2560], P(('inner', 'rep')), may hold values from -6 to 6
- momentum: float32 [5120, 2560], P(('inner', 'rep')), may hold values from -4 to 4
Outputs:
- weights_out: bfloat16 [5120, 2560], P('inner')
- master_out: float32 [5120, 2560], P(('inner', 'rep'))
- momentum_out: float32 [5120, 2560], P(('inner', 'rep'))
All inputs are finite; a program needn't handle non-finite values.
Results may differ from a plain program's by a relative error of at most 0.014.
Values may be sent and summed in bfloat16 or wider, within the bound.
No kernel may reach another device: no remote copies, remote signals or barrier semaphores. Data moves between devices by JAX's collectives and lax.ppermute only.
A program may use at most 64 MiB of HBM per device.

v0:
```python
import jax.numpy as jnp
from jax import lax

N_REP = 32


outer_rate = 0.7


momentum_decay = 0.9


def reference(deltas, master_weight, momentum):

    def accumulate(index, running):
        return running + deltas[index].astype(jnp.float32)

    summed = lax.fori_loop(0, N_REP, accumulate, jnp.zeros(master_weight.shape, jnp.float32))
    average = summed / N_REP
    momentum_out = momentum_decay * momentum + average
    master_out = master_weight - outer_rate * (average + momentum_decay * momentum_out)
    weights_out = master_out.astype(jnp.bfloat16)
    return (weights_out, master_out, momentum_out)


def solution(mesh):
    return reference
```

profile of v0, /device:TPU:32, one launch (start us, length us, event | category | flops | bytes accessed | tf_op | source)
XLA Modules:
  0.0 268.6 jit_solution(6877797390605178854)
XLA Ops:
  7.2 5.5 %reshape.29 = bf16[1,1,32,20,2560]{4,3,2,1,0:T(8,128)(2,1)} reshape(bf16[1,640,2560]{2,1,0:T(8,128)(2,1)} %param.3) | data formatting | bytes 6553600 | tf_op jit(solution)/call_exported
  12.7 13.3 %all-to-all-start = ((bf16[1,1,32,20,2560]{4,3,1,0,2:T(8,128)(2,1)}), bf16[1,1,32,20,2560]{4,3,1,0,2:T(8,128)(2,1)}, u32[]{:S(2)}, u32[]{:S(2)}) async-start(bf16[1,1,32,20,2560]{4,3,1,0,2:T(8,128)(2,1)} %bitcast.9), calls=%async_computation | async-start | bytes 7864320 | tf_op jit(solution)/call_exported
  26.0 91.7 %all-to-all-done = bf16[1,1,32,20,2560]{4,3,1,0,2:T(8,128)(2,1)} async-done(((bf16[1,1,32,20,2560]{4,3,1,0,2:T(8,128)(2,1)}), bf16[1,1,32,20,2560]{4,3,1,0,2:T(8,128)(2,1)}, u32[]{:S(2)}, u32[]{:S(2)}) %all-to-all-start) | async-done | bytes 3276832 | tf_op jit(solution)/call_exported
  117.8 31.8 %while.17 = (s32[]{:T(128)}, f32[20,2560]{1,0:T(8,128)S(1)}, bf16[1,640,2560]{2,1,0:T(8,128)(2,1)}, bf16[1,1,32,20,2560]{4,3,2,1,0:T(8,128)(2,1)}, s32[]{:T(128)}, /*index=5*/s32[]{:T(128)}) while((s32[]{:T(128)}, f32[20,2560]{1,0:T(8,128)S(1)}, bf16[1,640,2560]{2,1,0:T(8,128)(2,1)}, ...), condition=%wide.wide.region_1.0_spmd.clone, body=%wide.wide.region_0.0_spmd.clone.sunk | while | flops 153603 | bytes 512083 | solution.py:18
  118.8 1.0 convert_add_fusion.2
  119.8 1.0 convert_add_fusion.2
  120.8 1.0 convert_add_fusion.2
  121.8 1.0 convert_add_fusion.2
  122.7 1.0 convert_add_fusion.2
  123.7 1.0 convert_add_fusion.2
  124.7 1.0 convert_add_fusion.2
  125.7 1.0 convert_add_fusion.2
  126.7 1.0 convert_add_fusion.2
  128.7 1.0 convert_add_fusion.2
  129.7 1.0 convert_add_fusion.2
  130.7 1.0 convert_add_fusion.2
  131.7 1.0 convert_add_fusion.2
  132.7 1.0 convert_add_fusion.2
  133.7 1.0 convert_add_fusion.2
  134.7 1.0 convert_add_fusion.2
  135.7 1.0 convert_add_fusion.2
  136.7 1.0 convert_add_fusion.2
  137.7 1.0 convert_add_fusion.2
  138.7 1.0 convert_add_fusion.2
  139.7 1.0 convert_add_fusion.2
  141.7 1.0 convert_add_fusion.2
  143.7 1.0 convert_add_fusion.2
  145.7 1.0 convert_add_fusion.2
  147.6 1.0 convert_add_fusion.2
  148.6 1.0 convert_add_fusion.2
  150.5 105.7 %all-gather.4.cloned.1.call-done = bf16[32,20,2560]{2,1,0:T(8,128)(2,1)} async-done(((bf16[1,20,2560]{2,1,0:T(8,128)(2,1)}), bf16[32,20,2560]{2,1,0:T(8,128)(2,1)}) %all-gather.4.cloned.1.call-update) | async-done | bytes 3276816 | tf_op jit(solution)/convert_element_type | solution.py:22
  256.2 5.5 %reshape.26 = bf16[640,2560]{1,0:T(8,128)(2,1)} reshape(bf16[32,20,2560]{2,1,0:T(8,128)(2,1)} %all-gather.4.cloned.1.call-done) | data formatting | bytes 6553600
  (14 shorter events, 6.8 us)
Async XLA Ops:
  12.7 136.9 %copy-start = (f32[20,2560]{1,0:T(8,128)S(1)}, f32[20,2560]{1,0:T(8,128)}, u32[]{:S(2)}) copy-start(f32[20,2560]{1,0:T(8,128)} %param.2) | copy-start | bytes 614404
  12.7 137.0 %copy-start.1 = (f32[20,2560]{1,0:T(8,128)S(1)}, f32[20,2560]{1,0:T(8,128)}, u32[]{:S(2)}) copy-start(f32[20,2560]{1,0:T(8,128)} %param.4) | copy-start | bytes 614404
  12.7 105.1 %all-to-all-start = ((bf16[1,1,32,20,2560]{4,3,1,0,2:T(8,128)(2,1)}), bf16[1,1,32,20,2560]{4,3,1,0,2:T(8,128)(2,1)}, u32[]{:S(2)}, u32[]{:S(2)}) async-start(bf16[1,1,32,20,2560]{4,3,1,0,2:T(8,128)(2,1)} %bitcast.9), calls=%async_computation | async-start | bytes 7864320 | tf_op jit(solution)/call_exported
  26.0 230.2 %all-gather.4.cloned.1.call-start = ((), (), s32[]{:S(2)}) async-start(), calls=%async_computation.1 | async-start | bytes 4055040 | tf_op jit(solution)/convert_element_type | solution.py:22
Sparse Core Ops, SparseCore 0:
  150.7 105.5 all-gather.3
where the time goes:
time: 270 us; the launch traced here: 269 us
  waiting for transfers between devices  197 us (73%)
  other arithmetic  32.1 us (12%)
  between operations  14.1 us (5%)
  starting transfers between devices  13.3 us (5%)
  local copies, waits for them, and re-layouts  11.1 us (4%)
    convert_element_type x1, waiting for transfers between devices, reference(): weights_out = master_out.astype(jnp.bfloat16)  106 us
    another operation x1, waiting for transfers between devices  91.7 us
    add x32, other arithmetic, accumulate(): return running + deltas[index].astype(jnp.float32)  31.2 us
    another operation x1, starting transfers between devices  13.3 us
    unnamed x5, local copies, waits for them, and re-layouts  5.53 us
    another operation x1, local copies, waits for them, and re-layouts  5.52 us
  transfers between devices with their start and end apart: 2, of which 2 were waited for; matrix products, arithmetic and copies ran while one was open for 0% of the time, Pallas kernels for 0%

commit v1 on v0

v1 whole, which is shorter than its diff:
```python
import jax
import jax.numpy as jnp
from jax import lax
from jax.experimental import pallas as pl
from jax.experimental.pallas import tpu as pltpu
from jax.sharding import Mesh, PartitionSpec as P

N_REP = 32
OUTER_RATE = 0.7
DECAY = 0.9
AXES = ("zhi", "y", "x", "inner")
SIZES = (2, 4, 4, 8)
D = 2560
HALF = D // 2
ROWS = 20
BLOCK = 80
F32 = jnp.float32
BF16 = jnp.bfloat16


def shift_pairs(axis, step):
    at = AXES.index(axis)
    stride = 1
    for size in SIZES[at + 1:]:
        stride *= size
    total = 256
    pairs = []
    for device in range(total):
        place = device // stride % SIZES[at]
        pairs.append((device, device + ((place + step) % SIZES[at] - place) * stride))
    return pairs


def shifted(array, axis, step):
    return lax.ppermute(array, AXES, shift_pairs(axis, step))


def call(body, outs, *args, scratch=()):
    moved = sum(a.size * a.dtype.itemsize for a in (*args, *outs))
    return pl.pallas_call(
        body,
        out_shape=outs,
        in_specs=[pl.BlockSpec(memory_space=pltpu.VMEM)] * len(args),
        out_specs=[pl.BlockSpec(memory_space=pltpu.VMEM)] * len(outs),
        scratch_shapes=scratch,
        cost_estimate=pl.CostEstimate(flops=moved, bytes_accessed=moved, transcendentals=0),
        compiler_params=pltpu.CompilerParams(vmem_limit_bytes=40 * 2**20),
    )(*args)


def like(shape, dtype):
    return jax.ShapeDtypeStruct(shape, dtype)


def pack(d_ref, *out):
    x, y = lax.axis_index("x"), lax.axis_index("y")
    for s in range(4):
        for j in range(4):
            @pl.when(lax.rem(x + s, 4) == j)
            def _():
                for k in range(4):
                    out[s][pl.ds(ROWS * k, ROWS), :] = d_ref[k, pl.ds(ROWS * j, ROWS), :]
        out[4 + s][...] = d_ref[4 + lax.rem(y + s, 4)]


def narrow(value):
    return jnp.concatenate([value[:, :HALF], value[:, HALF:]], axis=0)


def wide(value):
    return jnp.concatenate([value[:ROWS], value[ROWS:]], axis=1)


def first_sum(*refs):
    parts, out, total = refs[:8], refs[8:16], refs[16]
    x, y = lax.axis_index("x"), lax.axis_index("y")
    for h, place in ((0, y), (1, x)):
        for k in range(4):
            rows = pl.ds(ROWS * k, ROWS)
            value = parts[4 * h][rows, :].astype(F32)
            for s in range(1, 4):
                value = value + parts[4 * h + s][rows, :].astype(F32)
            total[h, k] = value
        for s in range(4):
            value = total[h, lax.rem(place + s, 4)]
            o = out[4 * h + s]
            o[pl.ds(0, ROWS), :] = value[:, :HALF].astype(o.dtype)
            o[pl.ds(ROWS, ROWS), :] = value[:, HALF:].astype(o.dtype)


def second_sum(*refs):
    parts, out = refs[:8], refs[8]
    for h in range(2):
        value = parts[4 * h][...]
        for s in range(1, 4):
            value = value + parts[4 * h + s][...].astype(F32)
        out[h] = value.astype(BF16)


def update(own, other, base_own, base_other, momentum, weights, master_out, momentum_out):
    z = lax.axis_index("zhi")
    for h in range(2):
        average = (own[h].astype(F32) + other[h].astype(F32)) * (1.0 / N_REP)

        def halves(ref_base, row_average, col):
            return ref_base[:, col * HALF:(col + 1) * HALF] - (OUTER_RATE * (1 + DECAY)) * row_average

        for col in range(2):
            part = average[ROWS * col:ROWS * (col + 1)]
            cols = pl.ds(HALF * col, HALF)

            @pl.when(z == h)
            def _():
                momentum_out[:, cols] = DECAY * momentum[:, cols] + part
                new = base_own[:, cols] - (OUTER_RATE * (1 + DECAY)) * part
                master_out[:, cols] = new
                weights[h, pl.ds(ROWS * col, ROWS), :] = new.astype(BF16)

            @pl.when(z != h)
            def _():
                new = base_other[:, cols] - (OUTER_RATE * (1 + DECAY)) * part
                weights[h, pl.ds(ROWS * col, ROWS), :] = new.astype(BF16)


def join(weights, *refs):
    for h in range(2):
        out = refs[6 + h]
        out[0] = weights[h]
        for s in range(1, 4):
            out[s] = refs[3 * h + s - 1][...]


def unpack(*refs):
    parts, out = refs[:8], refs[8]
    x, y = lax.axis_index("x"), lax.axis_index("y")
    for s in range(4):
        for t in range(4):
            for j in range(4):
                @pl.when(lax.rem(x + 4 - t, 4) == j)
                def _():
                    row = lax.rem(y + 4 - s, 4)
                    for col in range(2):
                        out[row, pl.ds(ROWS * j, ROWS), pl.ds(HALF * col, HALF)] = parts[t][s, pl.ds(ROWS * col, ROWS), :]
                    row = 4 + lax.rem(y + 4 - s, 4)
                    for col in range(2):
                        out[row, pl.ds(ROWS * j, ROWS), pl.ds(HALF * col, HALF)] = parts[4 + s][t, pl.ds(ROWS * col, ROWS), :]


def local(deltas, master, momentum):
    d = deltas.reshape(8, BLOCK, D)
    packed = call(pack, [like((BLOCK, D), BF16)] * 8, d)
    a, b = list(packed[:4]), list(packed[4:])
    for s in (1, 3, 2):
        a[s] = shifted(packed[s], "x", s)
        b[s] = shifted(packed[4 + s], "y", s)
    base = master - (OUTER_RATE * DECAY * DECAY) * momentum
    base_other = shifted(base, "zhi", 1)

    small = (2 * ROWS, HALF)
    firsts = call(
        first_sum, ([like(small, F32)] + [like(small, BF16)] * 3) * 2, *a, *b,
        scratch=[pltpu.VMEM((2, 4, ROWS, D), F32)],
    )
    a, b = list(firsts[:4]), list(firsts[4:])
    for s in (1, 3, 2):
        a[s] = shifted(firsts[s], "y", s)
        b[s] = shifted(firsts[4 + s], "x", s)
    (own,) = call(second_sum, [like((2,) + small, BF16)], *a, *b)
    other = shifted(own, "zhi", 1)
    weights, master_out, momentum_out = call(
        update, [like((2,) + small, BF16), like((ROWS, D), F32), like((ROWS, D), F32)],
        own, other, base, base_other, momentum,
    )
    a = [shifted(weights[0], "y", s) for s in range(1, 4)]
    b = [shifted(weights[1], "x", s) for s in range(1, 4)]
    joined = call(join, [like((4,) + small, BF16)] * 2, weights, *a, *b)
    a = [joined[0]] + [shifted(joined[0], "x", s) for s in range(1, 4)]
    b = [joined[1]] + [shifted(joined[1], "y", s) for s in range(1, 4)]
    (out,) = call(unpack, [like((8, BLOCK, D), BF16)], *a, *b)
    return out.reshape(8 * BLOCK, D), master_out, momentum_out


def solution(mesh):
    parts = Mesh(mesh.devices.reshape(SIZES), AXES)
    rep = ("zhi", "y", "x")
    rows = P(("inner",) + rep, None)
    return jax.shard_map(
        local,
        mesh=parts,
        in_specs=(P(rep, "inner", None), rows, rows),
        out_specs=(P("inner", None), rows, rows),
        check_vma=False,
    )
```

time: 270 us -> 107 us (0.40)
  waiting for transfers between devices: 197 us -> 52.5 us
  starting transfers between devices: 13.3 us -> 45.5 us
  other arithmetic: 32.1 us -> 0.03 us
  between operations: 14.1 us -> 0.71 us
  local copies, waits for them, and re-layouts: 11.1 us -> 1.94 us
  Pallas kernels: 0 us -> 4.59 us
    convert_element_type x1 -> x0, waiting for transfers between devices: 106 us -> none  [reference(): weights_out = master_out.astype(jnp.bfloat16)]
    another operation x1 -> x0, waiting for transfers between devices: 91.7 us -> none
    ppermute x0 -> x26, waiting for transfers between devices: none -> 52.5 us  [shifted(): return lax.ppermute(array, AXES, shift_pairs(axis, step))]
    ppermute x0 -> x26, starting transfers between devices: none -> 45.5 us  [shifted(): return lax.ppermute(array, AXES, shift_pairs(axis, step))]
    add x32 -> x0, other arithmetic: 31.2 us -> none  [accumulate(): return running + deltas[index].astype(jnp.float32)]
    another operation x1 -> x0, starting transfers between devices: 13.3 us -> none
    another operation x1 -> x0, local copies, waits for them, and re-layouts: 5.52 us -> none
    pallas_call x0 -> x6, Pallas kernels: none -> 4.59 us  [call(): pl.pallas_call(body, out_shape=outs, in_specs=[pl.BlockSpec(memory_space=...]
  transfers between devices with their start and end apart: 2 -> 26, of which waited for: 2 -> 12; matrix products, arithmetic and copies ran while one was open for 0% -> 0% of each run, Pallas kernels for 0% -> 0%
where the time goes in v1:
time: 107 us; the launch traced here: 105 us
  waiting for transfers between devices  52.5 us (49%)
  starting transfers between devices  45.5 us (43%)
  Pallas kernels  4.59 us (4%)
  local copies, waits for them, and re-layouts  1.94 us (2%)
    ppermute x26, waiting for transfers between devices, shifted(): return lax.ppermute(array, AXES, shift_pairs(axis, step))  52.5 us
    ppermute x26, starting transfers between devices, shifted(): return lax.ppermute(array, AXES, shift_pairs(axis, step))  45.5 us
    pallas_call x6, Pallas kernels, call(): pl.pallas_call(body, out_shape=outs, in_specs=[pl.BlockSpec(memory_space=...  4.59 us
  transfers between devices with their start and end apart: 26, of which 12 were waited for; matrix products, arithmetic and copies ran while one was open for 0% of the time, Pallas kernels for 0%

profile of v1, /device:TPU:32, one launch (start us, length us, event | category | flops | bytes accessed | tf_op | source)
XLA Modules:
  0.0 105.2 jit_solution(10095481832516112103)
XLA Ops:
  0.6 1.9 %copy-done = bf16[1,640,2560]{2,1,0:T(8,128)(2,1)S(1)} copy-done((bf16[1,640,2560]{2,1,0:T(8,128)(2,1)S(1)}, bf16[1,640,2560]{2,1,0:T(8,128)(2,1)}, u32[]{:S(2)}) %copy-start) | copy-done | bytes 3276824
  2.9 1.6 %collective-permute-start = (bf16[80,2560]{1,0:T(8,128)(2,1)S(1)}, bf16[80,2560]{1,0:T(8,128)(2,1)S(1)}, u32[]{:S(2)}, u32[]{:S(2)}) collective-permute-start(bf16[80,2560]{1,0:T(8,128)(2,1)S(1)} %get-tuple-element.25), channel_id=1, source_target_pairs={{0,8},{1,9},{2,10},{3,11},{4,12},{5,13},{6,14},{7,15},{8,16},{9,17... | collective-permute-start | bytes 1228808 | tf_op jit(solution)/shard_map/ppermute | solution.py:35
  4.5 2.7 %collective-permute-start.1 = (bf16[80,2560]{1,0:T(8,128)(2,1)S(1)}, bf16[80,2560]{1,0:T(8,128)(2,1)S(1)}, u32[]{:S(2)}, u32[]{:S(2)}) collective-permute-start(bf16[80,2560]{1,0:T(8,128)(2,1)S(1)} %get-tuple-element.26), channel_id=1, source_target_pairs={{0,16},{1,17},{2,18},{3,19},{4,20},{5,21},{6,22},{7,23},{8,24},{9,... | collective-permute-start | bytes 1228808 | tf_op jit(solution)/shard_map/ppermute | solution.py:35
  7.2 1.4 %collective-permute-start.2 = (bf16[80,2560]{1,0:T(8,128)(2,1)S(1)}, bf16[80,2560]{1,0:T(8,128)(2,1)S(1)}, u32[]{:S(2)}, u32[]{:S(2)}) collective-permute-start(bf16[80,2560]{1,0:T(8,128)(2,1)S(1)} %get-tuple-element.27), channel_id=1, source_target_pairs={{0,24},{1,25},{2,26},{3,27},{4,28},{5,29},{6,30},{7,31},{8,0},{9,1... | collective-permute-start | bytes 1228808 | tf_op jit(solution)/shard_map/ppermute | solution.py:35
  8.6 1.6 %collective-permute-start.3 = (bf16[80,2560]{1,0:T(8,128)(2,1)S(1)}, bf16[80,2560]{1,0:T(8,128)(2,1)S(1)}, u32[]{:S(2)}, u32[]{:S(2)}) collective-permute-start(bf16[80,2560]{1,0:T(8,128)(2,1)S(1)} %get-tuple-element.29), channel_id=1, source_target_pairs={{0,32},{1,33},{2,34},{3,35},{4,36},{5,37},{6,38},{7,39},{8,40},{9,... | collective-permute-start | bytes 1228808 | tf_op jit(solution)/shard_map/ppermute | solution.py:35
  10.2 2.9 %collective-permute-start.4 = (bf16[80,2560]{1,0:T(8,128)(2,1)S(1)}, bf16[80,2560]{1,0:T(8,128)(2,1)S(1)}, u32[]{:S(2)}, u32[]{:S(2)}) collective-permute-start(bf16[80,2560]{1,0:T(8,128)(2,1)S(1)} %get-tuple-element.30), channel_id=1, source_target_pairs={{0,64},{1,65},{2,66},{3,67},{4,68},{5,69},{6,70},{7,71},{8,72},{9,... | collective-permute-start | bytes 1228808 | tf_op jit(solution)/shard_map/ppermute | solution.py:35
  13.1 2.5 %collective-permute-done.refs_1_ = bf16[80,2560]{1,0:T(8,128)(2,1)S(1)} collective-permute-done((bf16[80,2560]{1,0:T(8,128)(2,1)S(1)}, bf16[80,2560]{1,0:T(8,128)(2,1)S(1)}, u32[]{:S(2)}, u32[]{:S(2)}) %collective-permute-start) | collective-permute-done | bytes 409632 | tf_op jit(solution)/shard_map/ppermute | solution.py:35
  15.6 3.0 %collective-permute-start.5 = (bf16[80,2560]{1,0:T(8,128)(2,1)S(1)}, bf16[80,2560]{1,0:T(8,128)(2,1)S(1)}, u32[]{:S(2)}, u32[]{:S(2)}) collective-permute-start(bf16[80,2560]{1,0:T(8,128)(2,1)S(1)} %get-tuple-element.31), channel_id=1, source_target_pairs={{0,96},{1,97},{2,98},{3,99},{4,100},{5,101},{6,102},{7,103},{8,104... | collective-permute-start | bytes 1228808 | tf_op jit(solution)/shard_map/ppermute | solution.py:35
  18.6 6.6 %collective-permute-done.1.refs_2_ = bf16[80,2560]{1,0:T(8,128)(2,1)S(1)} collective-permute-done((bf16[80,2560]{1,0:T(8,128)(2,1)S(1)}, bf16[80,2560]{1,0:T(8,128)(2,1)S(1)}, u32[]{:S(2)}, u32[]{:S(2)}) %collective-permute-start.1) | collective-permute-done | bytes 409632 | tf_op jit(solution)/shard_map/ppermute | solution.py:35
  25.2 5.1 %collective-permute-done.4.refs_6_ = bf16[80,2560]{1,0:T(8,128)(2,1)S(1)} collective-permute-done((bf16[80,2560]{1,0:T(8,128)(2,1)S(1)}, bf16[80,2560]{1,0:T(8,128)(2,1)S(1)}, u32[]{:S(2)}, u32[]{:S(2)}) %collective-permute-start.4) | collective-permute-done | bytes 409632 | tf_op jit(solution)/shard_map/ppermute | solution.py:35
  31.1 2.0 %collective-permute-start.6 = (bf16[40,1280]{1,0:T(8,128)(2,1)S(1)}, bf16[40,1280]{1,0:T(8,128)(2,1)S(1)}, u32[]{:S(2)}, u32[]{:S(2)}) collective-permute-start(bf16[40,1280]{1,0:T(8,128)(2,1)S(1)} %get-tuple-element.33), channel_id=1, source_target_pairs={{0,32},{1,33},{2,34},{3,35},{4,36},{5,37},{6,38},{7,39},{8,40},{9,... | collective-permute-start | bytes 307208 | tf_op jit(solution)/shard_map/ppermute | solution.py:35
  33.1 1.6 %collective-permute-start.7 = (bf16[40,1280]{1,0:T(8,128)(2,1)S(1)}, bf16[40,1280]{1,0:T(8,128)(2,1)S(1)}, u32[]{:S(2)}, u32[]{:S(2)}) collective-permute-start(bf16[40,1280]{1,0:T(8,128)(2,1)S(1)} %get-tuple-element.34), channel_id=1, source_target_pairs={{0,64},{1,65},{2,66},{3,67},{4,68},{5,69},{6,70},{7,71},{8,72},{9,... | collective-permute-start | bytes 307208 | tf_op jit(solution)/shard_map/ppermute | solution.py:35
  34.7 1.7 %collective-permute-start.8 = (bf16[40,1280]{1,0:T(8,128)(2,1)S(1)}, bf16[40,1280]{1,0:T(8,128)(2,1)S(1)}, u32[]{:S(2)}, u32[]{:S(2)}) collective-permute-start(bf16[40,1280]{1,0:T(8,128)(2,1)S(1)} %get-tuple-element.35), channel_id=1, source_target_pairs={{0,96},{1,97},{2,98},{3,99},{4,100},{5,101},{6,102},{7,103},{8,104... | collective-permute-start | bytes 307208 | tf_op jit(solution)/shard_map/ppermute | solution.py:35
  36.9 1.1 %collective-permute-start.10 = (bf16[40,1280]{1,0:T(8,128)(2,1)S(1)}, bf16[40,1280]{1,0:T(8,128)(2,1)S(1)}, u32[]{:S(2)}, u32[]{:S(2)}) collective-permute-start(bf16[40,1280]{1,0:T(8,128)(2,1)S(1)} %get-tuple-element.38), channel_id=1, source_target_pairs={{0,16},{1,17},{2,18},{3,19},{4,20},{5,21},{6,22},{7,23},{8,24},{9,... | collective-permute-start | bytes 307208 | tf_op jit(solution)/shard_map/ppermute | solution.py:35
  38.1 1.6 %collective-permute-start.11 = (bf16[40,1280]{1,0:T(8,128)(2,1)S(1)}, bf16[40,1280]{1,0:T(8,128)(2,1)S(1)}, u32[]{:S(2)}, u32[]{:S(2)}) collective-permute-start(bf16[40,1280]{1,0:T(8,128)(2,1)S(1)} %get-tuple-element.39), channel_id=1, source_target_pairs={{0,24},{1,25},{2,26},{3,27},{4,28},{5,29},{6,30},{7,31},{8,0},{9,1... | collective-permute-start | bytes 307208 | tf_op jit(solution)/shard_map/ppermute | solution.py:35
  39.7 6.4 %collective-permute-start.13 = (f32[20,2560]{1,0:T(8,128)S(1)}, f32[20,2560]{1,0:T(8,128)S(1)}, u32[]{:S(2)}, u32[]{:S(2)}) collective-permute-start(f32[20,2560]{1,0:T(8,128)S(1)} %multiply_subtract_fusion.base_own), channel_id=1, source_target_pairs={{0,128},{1,129},{2,130},{3,131},{4,132},{5,133},{6,134},{7,135},{8... | collective-permute-start | bytes 614408 | tf_op jit(solution)/shard_map/ppermute | solution.py:35
  46.2 4.5 %collective-permute-start.12 = (bf16[2,40,1280]{2,1,0:T(8,128)(2,1)S(1)}, bf16[2,40,1280]{2,1,0:T(8,128)(2,1)S(1)}, u32[]{:S(2)}, u32[]{:S(2)}) collective-permute-start(bf16[2,40,1280]{2,1,0:T(8,128)(2,1)S(1)} %shard_map.60.own), channel_id=1, source_target_pairs={{0,128},{1,129},{2,130},{3,131},{4,132},{5,133},{6,134},{7,135},{8... | collective-permute-start | bytes 614408 | tf_op jit(solution)/shard_map/ppermute | solution.py:35
  50.7 11.8 %collective-permute-done.13.base_other = f32[20,2560]{1,0:T(8,128)S(1)} collective-permute-done((f32[20,2560]{1,0:T(8,128)S(1)}, f32[20,2560]{1,0:T(8,128)S(1)}, u32[]{:S(2)}, u32[]{:S(2)}) %collective-permute-start.13) | collective-permute-done | bytes 204832 | tf_op jit(solution)/shard_map/ppermute | solution.py:35
  62.5 2.8 %collective-permute-done.12.other = bf16[2,40,1280]{2,1,0:T(8,128)(2,1)S(1)} collective-permute-done((bf16[2,40,1280]{2,1,0:T(8,128)(2,1)S(1)}, bf16[2,40,1280]{2,1,0:T(8,128)(2,1)S(1)}, u32[]{:S(2)}, u32[]{:S(2)}) %collective-permute-start.12) | collective-permute-done | bytes 204832 | tf_op jit(solution)/shard_map/ppermute | solution.py:35
  65.3 1.0 shard_map.61
  67.0 2.2 %collective-permute-start.18 = (bf16[40,1280]{1,0:T(8,128)(2,1)S(1)}, bf16[40,1280]{1,0:T(8,128)(2,1)S(1)}, u32[]{:S(2)}, u32[]{:S(2)}) collective-permute-start(bf16[40,1280]{1,0:T(8,128)(2,1)S(1)} %get-tuple-element.45), channel_id=1, source_target_pairs={{0,16},{1,17},{2,18},{3,19},{4,20},{5,21},{6,22},{7,23},{8,24},{9,... | collective-permute-start | bytes 307208 | tf_op jit(solution)/shard_map/ppermute | solution.py:35
  69.9 1.1 collective-permute-start.16
  73.2 1.9 %collective-permute-done.17.refs_3_ = bf16[40,1280]{1,0:T(8,128)(2,1)S(1)} collective-permute-done((bf16[40,1280]{1,0:T(8,128)(2,1)S(1)}, bf16[40,1280]{1,0:T(8,128)(2,1)S(1)}, u32[]{:S(2)}, u32[]{:S(2)}) %collective-permute-start.17) | collective-permute-done | bytes 102432 | tf_op jit(solution)/shard_map/ppermute | solution.py:35
  75.0 2.2 %collective-permute-done.15.refs_1_ = bf16[40,1280]{1,0:T(8,128)(2,1)S(1)} collective-permute-done((bf16[40,1280]{1,0:T(8,128)(2,1)S(1)}, bf16[40,1280]{1,0:T(8,128)(2,1)S(1)}, u32[]{:S(2)}, u32[]{:S(2)}) %collective-permute-start.15) | collective-permute-done | bytes 102432 | tf_op jit(solution)/shard_map/ppermute | solution.py:35
  77.2 1.0 collective-permute-done.14.refs_0_
  78.3 2.2 %collective-permute-start.22 = (bf16[4,40,1280]{2,1,0:T(8,128)(2,1)S(1)}, bf16[4,40,1280]{2,1,0:T(8,128)(2,1)S(1)}, u32[]{:S(2)}, u32[]{:S(2)}) collective-permute-start(bf16[4,40,1280]{2,1,0:T(8,128)(2,1)S(1)} %get-tuple-element.41.refs_0_), channel_id=1, source_target_pairs={{0,24},{1,25},{2,26},{3,27},{4,28},{5,29},{6,30},{7,31},{8,0},{9,1... | collective-permute-start | bytes 1228808 | tf_op jit(solution)/shard_map/ppermute | solution.py:35
  81.0 1.2 %collective-permute-start.20 = (bf16[4,40,1280]{2,1,0:T(8,128)(2,1)S(1)}, bf16[4,40,1280]{2,1,0:T(8,128)(2,1)S(1)}, u32[]{:S(2)}, u32[]{:S(2)}) collective-permute-start(bf16[4,40,1280]{2,1,0:T(8,128)(2,1)S(1)} %get-tuple-element.41.refs_0_), channel_id=1, source_target_pairs={{0,8},{1,9},{2,10},{3,11},{4,12},{5,13},{6,14},{7,15},{8,16},{9,17... | collective-permute-start | bytes 1228808 | tf_op jit(solution)/shard_map/ppermute | solution.py:35
  82.1 1.5 %collective-permute-start.25 = (bf16[4,40,1280]{2,1,0:T(8,128)(2,1)S(1)}, bf16[4,40,1280]{2,1,0:T(8,128)(2,1)S(1)}, u32[]{:S(2)}, u32[]{:S(2)}) collective-permute-start(bf16[4,40,1280]{2,1,0:T(8,128)(2,1)S(1)} %get-tuple-element.42.refs_4_), channel_id=1, source_target_pairs={{0,96},{1,97},{2,98},{3,99},{4,100},{5,101},{6,102},{7,103},{8,104... | collective-permute-start | bytes 1228808 | tf_op jit(solution)/shard_map/ppermute | solution.py:35
  84.5 9.3 %collective-permute-done.22.refs_3_ = bf16[4,40,1280]{2,1,0:T(8,128)(2,1)S(1)} collective-permute-done((bf16[4,40,1280]{2,1,0:T(8,128)(2,1)S(1)}, bf16[4,40,1280]{2,1,0:T(8,128)(2,1)S(1)}, u32[]{:S(2)}, u32[]{:S(2)}) %collective-permute-start.22) | collective-permute-done | bytes 409632 | tf_op jit(solution)/shard_map/ppermute | solution.py:35
  94.2 3.2 %collective-permute-done.20.refs_1_ = bf16[4,40,1280]{2,1,0:T(8,128)(2,1)S(1)} collective-permute-done((bf16[4,40,1280]{2,1,0:T(8,128)(2,1)S(1)}, bf16[4,40,1280]{2,1,0:T(8,128)(2,1)S(1)}, u32[]{:S(2)}, u32[]{:S(2)}) %collective-permute-start.20) | collective-permute-done | bytes 409632 | tf_op jit(solution)/shard_map/ppermute | solution.py:35
  97.5 5.5 %collective-permute-done.23.refs_5_ = bf16[4,40,1280]{2,1,0:T(8,128)(2,1)S(1)} collective-permute-done((bf16[4,40,1280]{2,1,0:T(8,128)(2,1)S(1)}, bf16[4,40,1280]{2,1,0:T(8,128)(2,1)S(1)}, u32[]{:S(2)}, u32[]{:S(2)}) %collective-permute-start.23) | collective-permute-done | bytes 409632 | tf_op jit(solution)/shard_map/ppermute | solution.py:35
  102.9 2.3 %shard_map.63 = bf16[8,80,2560]{2,1,0:T(8,128)(2,1)} custom-call(bf16[4,40,1280]{2,1,0:T(8,128)(2,1)S(1)} %get-tuple-element.41.refs_0_, bf16[4,40,1280]{2,1,0:T(8,128)(2,1)S(1)} %collective-permute-done.20.refs_1_, bf16[4,40,1280]{2,1,0:T(8,128)(2,1)S(1)} %collective-permute-done.21.refs_2_, bf16[4,40,1280]{2,1,0:T(8,128)(2,1)S(1)} %collective-permute-done.22.refs_3_, ...), custom_call_target="tpu_custom_call" | custom-call | flops 6553600 | bytes 6553600 | tf_op jit(solution)/shard_map/pallas_call | solution.py:40
  (34 shorter events, 7.5 us)
Async XLA Ops:
  0.6 1.9 %copy-start = (bf16[1,640,2560]{2,1,0:T(8,128)(2,1)S(1)}, bf16[1,640,2560]{2,1,0:T(8,128)(2,1)}, u32[]{:S(2)}) copy-start(bf16[1,640,2560]{2,1,0:T(8,128)(2,1)} %param.3) | copy-start | bytes 9830404
  2.6 37.1 %copy-start.1 = (f32[20,2560]{1,0:T(8,128)S(1)}, f32[20,2560]{1,0:T(8,128)}, u32[]{:S(2)}) copy-start(f32[20,2560]{1,0:T(8,128)} %momentum.1) | copy-start | bytes 614404
  2.6 37.1 %copy-start.2 = (f32[20,2560]{1,0:T(8,128)S(1)}, f32[20,2560]{1,0:T(8,128)}, u32[]{:S(2)}) copy-start(f32[20,2560]{1,0:T(8,128)} %param.4) | copy-start | bytes 614404
  2.9 12.7 %collective-permute-start = (bf16[80,2560]{1,0:T(8,128)(2,1)S(1)}, bf16[80,2560]{1,0:T(8,128)(2,1)S(1)}, u32[]{:S(2)}, u32[]{:S(2)}) collective-permute-start(bf16[80,2560]{1,0:T(8,128)(2,1)S(1)} %get-tuple-element.25), channel_id=1, source_target_pairs={{0,8},{1,9},{2,10},{3,11},{4,12},{5,13},{6,14},{7,15},{8,16},{9,17... | collective-permute-start | bytes 1228808 | tf_op jit(solution)/shard_map/ppermute | solution.py:35
  4.5 20.7 %collective-permute-start.1 = (bf16[80,2560]{1,0:T(8,128)(2,1)S(1)}, bf16[80,2560]{1,0:T(8,128)(2,1)S(1)}, u32[]{:S(2)}, u32[]{:S(2)}) collective-permute-start(bf16[80,2560]{1,0:T(8,128)(2,1)S(1)} %get-tuple-element.26), channel_id=1, source_target_pairs={{0,16},{1,17},{2,18},{3,19},{4,20},{5,21},{6,22},{7,23},{8,24},{9,... | collective-permute-start | bytes 1228808 | tf_op jit(solution)/shard_map/ppermute | solution.py:35
  7.2 18.0 %collective-permute-start.2 = (bf16[80,2560]{1,0:T(8,128)(2,1)S(1)}, bf16[80,2560]{1,0:T(8,128)(2,1)S(1)}, u32[]{:S(2)}, u32[]{:S(2)}) collective-permute-start(bf16[80,2560]{1,0:T(8,128)(2,1)S(1)} %get-tuple-element.27), channel_id=1, source_target_pairs={{0,24},{1,25},{2,26},{3,27},{4,28},{5,29},{6,30},{7,31},{8,0},{9,1... | collective-permute-start | bytes 1228808 | tf_op jit(solution)/shard_map/ppermute | solution.py:35
  8.6 16.5 %collective-permute-start.3 = (bf16[80,2560]{1,0:T(8,128)(2,1)S(1)}, bf16[80,2560]{1,0:T(8,128)(2,1)S(1)}, u32[]{:S(2)}, u32[]{:S(2)}) collective-permute-start(bf16[80,2560]{1,0:T(8,128)(2,1)S(1)} %get-tuple-element.29), channel_id=1, source_target_pairs={{0,32},{1,33},{2,34},{3,35},{4,36},{5,37},{6,38},{7,39},{8,40},{9,... | collective-permute-start | bytes 1228808 | tf_op jit(solution)/shard_map/ppermute | solution.py:35
  10.2 20.0 %collective-permute-start.4 = (bf16[80,2560]{1,0:T(8,128)(2,1)S(1)}, bf16[80,2560]{1,0:T(8,128)(2,1)S(1)}, u32[]{:S(2)}, u32[]{:S(2)}) collective-permute-start(bf16[80,2560]{1,0:T(8,128)(2,1)S(1)} %get-tuple-element.30), channel_id=1, source_target_pairs={{0,64},{1,65},{2,66},{3,67},{4,68},{5,69},{6,70},{7,71},{8,72},{9,... | collective-permute-start | bytes 1228808 | tf_op jit(solution)/shard_map/ppermute | solution.py:35
  15.6 14.7 %collective-permute-start.5 = (bf16[80,2560]{1,0:T(8,128)(2,1)S(1)}, bf16[80,2560]{1,0:T(8,128)(2,1)S(1)}, u32[]{:S(2)}, u32[]{:S(2)}) collective-permute-start(bf16[80,2560]{1,0:T(8,128)(2,1)S(1)} %get-tuple-element.31), channel_id=1, source_target_pairs={{0,96},{1,97},{2,98},{3,99},{4,100},{5,101},{6,102},{7,103},{8,104... | collective-permute-start | bytes 1228808 | tf_op jit(solution)/shard_map/ppermute | solution.py:35
  31.1 7.0 %collective-permute-start.6 = (bf16[40,1280]{1,0:T(8,128)(2,1)S(1)}, bf16[40,1280]{1,0:T(8,128)(2,1)S(1)}, u32[]{:S(2)}, u32[]{:S(2)}) collective-permute-start(bf16[40,1280]{1,0:T(8,128)(2,1)S(1)} %get-tuple-element.33), channel_id=1, source_target_pairs={{0,32},{1,33},{2,34},{3,35},{4,36},{5,37},{6,38},{7,39},{8,40},{9,... | collective-permute-start | bytes 307208 | tf_op jit(solution)/shard_map/ppermute | solution.py:35
  33.1 6.6 %collective-permute-start.7 = (bf16[40,1280]{1,0:T(8,128)(2,1)S(1)}, bf16[40,1280]{1,0:T(8,128)(2,1)S(1)}, u32[]{:S(2)}, u32[]{:S(2)}) collective-permute-start(bf16[40,1280]{1,0:T(8,128)(2,1)S(1)} %get-tuple-element.34), channel_id=1, source_target_pairs={{0,64},{1,65},{2,66},{3,67},{4,68},{5,69},{6,70},{7,71},{8,72},{9,... | collective-permute-start | bytes 307208 | tf_op jit(solution)/shard_map/ppermute | solution.py:35
  34.7 11.4 %collective-permute-start.8 = (bf16[40,1280]{1,0:T(8,128)(2,1)S(1)}, bf16[40,1280]{1,0:T(8,128)(2,1)S(1)}, u32[]{:S(2)}, u32[]{:S(2)}) collective-permute-start(bf16[40,1280]{1,0:T(8,128)(2,1)S(1)} %get-tuple-element.35), channel_id=1, source_target_pairs={{0,96},{1,97},{2,98},{3,99},{4,100},{5,101},{6,102},{7,103},{8,104... | collective-permute-start | bytes 307208 | tf_op jit(solution)/shard_map/ppermute | solution.py:35
  36.4 9.7 %collective-permute-start.9 = (bf16[40,1280]{1,0:T(8,128)(2,1)S(1)}, bf16[40,1280]{1,0:T(8,128)(2,1)S(1)}, u32[]{:S(2)}, u32[]{:S(2)}) collective-permute-start(bf16[40,1280]{1,0:T(8,128)(2,1)S(1)} %get-tuple-element.37), channel_id=1, source_target_pairs={{0,8},{1,9},{2,10},{3,11},{4,12},{5,13},{6,14},{7,15},{8,16},{9,17... | collective-permute-start | bytes 307208 | tf_op jit(solution)/shard_map/ppermute | solution.py:35
  36.9 9.1 %collective-permute-start.10 = (bf16[40,1280]{1,0:T(8,128)(2,1)S(1)}, bf16[40,1280]{1,0:T(8,128)(2,1)S(1)}, u32[]{:S(2)}, u32[]{:S(2)}) collective-permute-start(bf16[40,1280]{1,0:T(8,128)(2,1)S(1)} %get-tuple-element.38), channel_id=1, source_target_pairs={{0,16},{1,17},{2,18},{3,19},{4,20},{5,21},{6,22},{7,23},{8,24},{9,... | collective-permute-start | bytes 307208 | tf_op jit(solution)/shard_map/ppermute | solution.py:35
  38.1 8.0 %collective-permute-start.11 = (bf16[40,1280]{1,0:T(8,128)(2,1)S(1)}, bf16[40,1280]{1,0:T(8,128)(2,1)S(1)}, u32[]{:S(2)}, u32[]{:S(2)}) collective-permute-start(bf16[40,1280]{1,0:T(8,128)(2,1)S(1)} %get-tuple-element.39), channel_id=1, source_target_pairs={{0,24},{1,25},{2,26},{3,27},{4,28},{5,29},{6,30},{7,31},{8,0},{9,1... | collective-permute-start | bytes 307208 | tf_op jit(solution)/shard_map/ppermute | solution.py:35
  39.7 22.8 %collective-permute-start.13 = (f32[20,2560]{1,0:T(8,128)S(1)}, f32[20,2560]{1,0:T(8,128)S(1)}, u32[]{:S(2)}, u32[]{:S(2)}) collective-permute-start(f32[20,2560]{1,0:T(8,128)S(1)} %multiply_subtract_fusion.base_own), channel_id=1, source_target_pairs={{0,128},{1,129},{2,130},{3,131},{4,132},{5,133},{6,134},{7,135},{8... | collective-permute-start | bytes 614408 | tf_op jit(solution)/shard_map/ppermute | solution.py:35
  46.2 19.1 %collective-permute-start.12 = (bf16[2,40,1280]{2,1,0:T(8,128)(2,1)S(1)}, bf16[2,40,1280]{2,1,0:T(8,128)(2,1)S(1)}, u32[]{:S(2)}, u32[]{:S(2)}) collective-permute-start(bf16[2,40,1280]{2,1,0:T(8,128)(2,1)S(1)} %shard_map.60.own), channel_id=1, source_target_pairs={{0,128},{1,129},{2,130},{3,131},{4,132},{5,133},{6,134},{7,135},{8... | collective-permute-start | bytes 614408 | tf_op jit(solution)/shard_map/ppermute | solution.py:35
  66.3 5.3 %collective-permute-start.19 = (bf16[40,1280]{1,0:T(8,128)(2,1)S(1)}, bf16[40,1280]{1,0:T(8,128)(2,1)S(1)}, u32[]{:S(2)}, u32[]{:S(2)}) collective-permute-start(bf16[40,1280]{1,0:T(8,128)(2,1)S(1)} %get-tuple-element.45), channel_id=1, source_target_pairs={{0,24},{1,25},{2,26},{3,27},{4,28},{5,29},{6,30},{7,31},{8,0},{9,1... | collective-permute-start | bytes 307208 | tf_op jit(solution)/shard_map/ppermute | solution.py:35
  67.0 6.2 %collective-permute-start.18 = (bf16[40,1280]{1,0:T(8,128)(2,1)S(1)}, bf16[40,1280]{1,0:T(8,128)(2,1)S(1)}, u32[]{:S(2)}, u32[]{:S(2)}) collective-permute-start(bf16[40,1280]{1,0:T(8,128)(2,1)S(1)} %get-tuple-element.45), channel_id=1, source_target_pairs={{0,16},{1,17},{2,18},{3,19},{4,20},{5,21},{6,22},{7,23},{8,24},{9,... | collective-permute-start | bytes 307208 | tf_op jit(solution)/shard_map/ppermute | solution.py:35
  69.2 5.9 %collective-permute-start.17 = (bf16[40,1280]{1,0:T(8,128)(2,1)S(1)}, bf16[40,1280]{1,0:T(8,128)(2,1)S(1)}, u32[]{:S(2)}, u32[]{:S(2)}) collective-permute-start(bf16[40,1280]{1,0:T(8,128)(2,1)S(1)} %get-tuple-element.45), channel_id=1, source_target_pairs={{0,8},{1,9},{2,10},{3,11},{4,12},{5,13},{6,14},{7,15},{8,16},{9,17... | collective-permute-start | bytes 307208 | tf_op jit(solution)/shard_map/ppermute | solution.py:35
  69.9 5.1 %collective-permute-start.16 = (bf16[40,1280]{1,0:T(8,128)(2,1)S(1)}, bf16[40,1280]{1,0:T(8,128)(2,1)S(1)}, u32[]{:S(2)}, u32[]{:S(2)}) collective-permute-start(bf16[40,1280]{1,0:T(8,128)(2,1)S(1)} %get-tuple-element.46), channel_id=1, source_target_pairs={{0,96},{1,97},{2,98},{3,99},{4,100},{5,101},{6,102},{7,103},{8,104... | collective-permute-start | bytes 307208 | tf_op jit(solution)/shard_map/ppermute | solution.py:35
  71.0 6.2 %collective-permute-start.15 = (bf16[40,1280]{1,0:T(8,128)(2,1)S(1)}, bf16[40,1280]{1,0:T(8,128)(2,1)S(1)}, u32[]{:S(2)}, u32[]{:S(2)}) collective-permute-start(bf16[40,1280]{1,0:T(8,128)(2,1)S(1)} %get-tuple-element.46), channel_id=1, source_target_pairs={{0,64},{1,65},{2,66},{3,67},{4,68},{5,69},{6,70},{7,71},{8,72},{9,... | collective-permute-start | bytes 307208 | tf_op jit(solution)/shard_map/ppermute | solution.py:35
  71.6 6.6 %collective-permute-start.14 = (bf16[40,1280]{1,0:T(8,128)(2,1)S(1)}, bf16[40,1280]{1,0:T(8,128)(2,1)S(1)}, u32[]{:S(2)}, u32[]{:S(2)}) collective-permute-start(bf16[40,1280]{1,0:T(8,128)(2,1)S(1)} %get-tuple-element.46), channel_id=1, source_target_pairs={{0,32},{1,33},{2,34},{3,35},{4,36},{5,37},{6,38},{7,39},{8,40},{9,... | collective-permute-start | bytes 307208 | tf_op jit(solution)/shard_map/ppermute | solution.py:35
  78.3 15.5 %collective-permute-start.22 = (bf16[4,40,1280]{2,1,0:T(8,128)(2,1)S(1)}, bf16[4,40,1280]{2,1,0:T(8,128)(2,1)S(1)}, u32[]{:S(2)}, u32[]{:S(2)}) collective-permute-start(bf16[4,40,1280]{2,1,0:T(8,128)(2,1)S(1)} %get-tuple-element.41.refs_0_), channel_id=1, source_target_pairs={{0,24},{1,25},{2,26},{3,27},{4,28},{5,29},{6,30},{7,31},{8,0},{9,1... | collective-permute-start | bytes 1228808 | tf_op jit(solution)/shard_map/ppermute | solution.py:35
  80.5 13.7 %collective-permute-start.21 = (bf16[4,40,1280]{2,1,0:T(8,128)(2,1)S(1)}, bf16[4,40,1280]{2,1,0:T(8,128)(2,1)S(1)}, u32[]{:S(2)}, u32[]{:S(2)}) collective-permute-start(bf16[4,40,1280]{2,1,0:T(8,128)(2,1)S(1)} %get-tuple-element.41.refs_0_), channel_id=1, source_target_pairs={{0,16},{1,17},{2,18},{3,19},{4,20},{5,21},{6,22},{7,23},{8,24},{9,... | collective-permute-start | bytes 1228808 | tf_op jit(solution)/shard_map/ppermute | solution.py:35
  81.0 16.5 %collective-permute-start.20 = (bf16[4,40,1280]{2,1,0:T(8,128)(2,1)S(1)}, bf16[4,40,1280]{2,1,0:T(8,128)(2,1)S(1)}, u32[]{:S(2)}, u32[]{:S(2)}) collective-permute-start(bf16[4,40,1280]{2,1,0:T(8,128)(2,1)S(1)} %get-tuple-element.41.refs_0_), channel_id=1, source_target_pairs={{0,8},{1,9},{2,10},{3,11},{4,12},{5,13},{6,14},{7,15},{8,16},{9,17... | collective-permute-start | bytes 1228808 | tf_op jit(solution)/shard_map/ppermute | solution.py:35
  82.1 15.3 %collective-permute-start.25 = (bf16[4,40,1280]{2,1,0:T(8,128)(2,1)S(1)}, bf16[4,40,1280]{2,1,0:T(8,128)(2,1)S(1)}, u32[]{:S(2)}, u32[]{:S(2)}) collective-permute-start(bf16[4,40,1280]{2,1,0:T(8,128)(2,1)S(1)} %get-tuple-element.42.refs_4_), channel_id=1, source_target_pairs={{0,96},{1,97},{2,98},{3,99},{4,100},{5,101},{6,102},{7,103},{8,104... | collective-permute-start | bytes 1228808 | tf_op jit(solution)/shard_map/ppermute | solution.py:35
  83.6 13.8 %collective-permute-start.24 = (bf16[4,40,1280]{2,1,0:T(8,128)(2,1)S(1)}, bf16[4,40,1280]{2,1,0:T(8,128)(2,1)S(1)}, u32[]{:S(2)}, u32[]{:S(2)}) collective-permute-start(bf16[4,40,1280]{2,1,0:T(8,128)(2,1)S(1)} %get-tuple-element.42.refs_4_), channel_id=1, source_target_pairs={{0,64},{1,65},{2,66},{3,67},{4,68},{5,69},{6,70},{7,71},{8,72},{9,... | collective-permute-start | bytes 1228808 | tf_op jit(solution)/shard_map/ppermute | solution.py:35
  93.8 9.2 %collective-permute-start.23 = (bf16[4,40,1280]{2,1,0:T(8,128)(2,1)S(1)}, bf16[4,40,1280]{2,1,0:T(8,128)(2,1)S(1)}, u32[]{:S(2)}, u32[]{:S(2)}) collective-permute-start(bf16[4,40,1280]{2,1,0:T(8,128)(2,1)S(1)} %get-tuple-element.42.refs_4_), channel_id=1, source_target_pairs={{0,32},{1,33},{2,34},{3,35},{4,36},{5,37},{6,38},{7,39},{8,40},{9,... | collective-permute-start | bytes 1228808 | tf_op jit(solution)/shard_map/ppermute | solution.py:35

commit v2 on v0

v2 whole, which is shorter than its diff:
```python
import functools

import jax
import jax.numpy as jnp
from jax import lax
from jax.experimental import pallas as pl
from jax.experimental.pallas import tpu as pltpu
from jax.sharding import Mesh, PartitionSpec as P

N_REP = 32
OUTER_RATE = 0.7
DECAY = 0.9
SCALE = OUTER_RATE * (1 + DECAY)
AXES = ("zhi", "y", "x", "inner")
SIZES = (2, 4, 4, 8)
D = 2560
HALF = D // 2
ROWS = 20
BLOCK = 80
SMALL = (2 * ROWS, HALF)
FOUR = (4,) + SMALL
F32 = jnp.float32
BF16 = jnp.bfloat16
ANY = pl.BlockSpec(memory_space=pl.ANY)
HBM = pl.BlockSpec(memory_space=pltpu.HBM)
VMEM = pl.BlockSpec(memory_space=pltpu.VMEM)
FIRST = (1, 3, 2)
MIDDLE = (1, 3, 2)
GATHER = (2, 3, 1)
LAST = (2, 3, 1)


def moved(array, axis, place):
    at = AXES.index(axis)
    stride = 1
    for size in SIZES[at + 1:]:
        stride *= size
    pairs = []
    for device in range(256):
        p = device // stride % SIZES[at]
        pairs.append((device, device + (place(p) - p) * stride))
    return lax.ppermute(array, AXES, pairs)


def shifted(array, axis, step):
    return moved(array, axis, lambda p: (p + step) % SIZES[AXES.index(axis)])


def swapped(array, axis, mask):
    return moved(array, axis, lambda p: p ^ mask)


def received(parts, axis, order):
    return [parts[0]] + [shifted(parts[s], axis, s) for s in order]


def call(body, outs, *args, scratch=(), aliases=None, specs=None, after=()):
    size = sum(a.size * a.dtype.itemsize for a in (*args, *outs))
    in_specs, out_specs = specs or ([VMEM] * len(args), [VMEM] * len(outs))
    count = len(args)
    args = (*args, *after)

    def kernel(*refs):
        body(*refs[:count], *refs[len(args):])

    return pl.pallas_call(
        kernel,
        out_shape=outs,
        in_specs=in_specs + [ANY] * len(after),
        out_specs=out_specs,
        scratch_shapes=scratch,
        input_output_aliases=aliases or {},
        cost_estimate=pl.CostEstimate(flops=size, bytes_accessed=size, transcendentals=0),
        compiler_params=pltpu.CompilerParams(vmem_limit_bytes=40 * 2**20),
    )(*args)


def like(shape, dtype):
    return jax.ShapeDtypeStruct(shape, dtype)


def pack_rows(d_ref, *out):
    x = lax.axis_index("x")
    for s in range(4):
        for j in range(4):
            @pl.when(lax.rem(x + s, 4) == j)
            def _():
                for k in range(4):
                    out[s][pl.ds(ROWS * k, ROWS), :] = d_ref[k, pl.ds(ROWS * j, ROWS), :]


def first_sum(axis, *refs):
    parts, out, total = refs[:4], refs[4:8], refs[8]
    place = lax.axis_index(axis)
    for k in range(4):
        rows = pl.ds(ROWS * k, ROWS)
        value = parts[0][rows, :].astype(F32)
        for s in range(1, 4):
            value = value + parts[s][rows, :].astype(F32)
        total[k] = value
    for s in range(4):
        value = total[lax.rem(place + s, 4)]
        o = out[s]
        for col in range(2):
            o[pl.ds(ROWS * col, ROWS), :] = value[:, HALF * col:HALF * (col + 1)].astype(o.dtype)


def second_sum(*refs):
    value = refs[0][...]
    for part in refs[1:4]:
        value = value + part[...].astype(F32)
    refs[4][...] = value.astype(BF16)


def early_base(master, momentum, base):
    base[...] = master[...] - (OUTER_RATE * DECAY * DECAY) * momentum[...]


def new_rows(owner, own, other, base_own, base_other, weights):
    mine = lax.axis_index("zhi") == owner
    for col in range(2):
        rows, cols = pl.ds(ROWS * col, ROWS), pl.ds(HALF * col, HALF)
        average = (own[rows, :].astype(F32) + other[rows, :].astype(F32)) * (1.0 / N_REP)
        base = jnp.where(mine, base_own[:, cols], base_other[:, cols])
        weights[rows, :] = (base - SCALE * average).astype(BF16)


def new_state(own_a, other_a, own_b, other_b, base, momentum, master_out, momentum_out):
    first = lax.axis_index("zhi") == 1
    for col in range(2):
        rows, cols = pl.ds(ROWS * col, ROWS), pl.ds(HALF * col, HALF)
        own = jnp.where(first, own_a[rows, :].astype(F32), own_b[rows, :].astype(F32))
        other = jnp.where(first, other_a[rows, :].astype(F32), other_b[rows, :].astype(F32))
        average = (own + other) * (1.0 / N_REP)
        momentum_out[:, cols] = DECAY * momentum[:, cols] + average
        master_out[:, cols] = base[:, cols] - SCALE * average


def join(*refs):
    for h in range(2):
        for part, s in enumerate((0,) + GATHER):
            refs[8 + h][s] = refs[4 * h + part][...]


def unpack_rows(*refs):
    parts, out, block, sems = refs[:4], refs[4], refs[5], refs[6]
    x, y = lax.axis_index("x"), lax.axis_index("y")
    copies = []
    for i in range(4):
        for part, t in enumerate((0,) + LAST):
            for j in range(4):
                @pl.when(lax.rem(x + 4 - t, 4) == j)
                def _():
                    for col in range(2):
                        block[i, pl.ds(ROWS * j, ROWS), pl.ds(HALF * col, HALF)] = parts[part][i, pl.ds(ROWS * col, ROWS), :]
        copies.append(pltpu.make_async_copy(block.at[i], out.at[lax.rem(y + 4 - i, 4)], sems.at[i]))
        copies[-1].start()
    for copy in copies:
        copy.wait()


def unpack_blocks(steps, *refs):
    count = len(steps)
    parts, out, block, sems = refs[:count], refs[count + 1], refs[count + 2], refs[count + 3]
    x, y = lax.axis_index("x"), lax.axis_index("y")
    copies = []
    for part, t in enumerate(steps):
        for i in range(4):
            for j in range(4):
                @pl.when(lax.rem(x + 4 - i, 4) == j)
                def _():
                    for col in range(2):
                        block[part, pl.ds(ROWS * j, ROWS), pl.ds(HALF * col, HALF)] = parts[part][i, pl.ds(ROWS * col, ROWS), :]
        copies.append(pltpu.make_async_copy(block.at[part], out.at[4 + lax.rem(y + 4 - t, 4)], sems.at[part]))
        copies[-1].start()
    for copy in copies:
        copy.wait()


def local(deltas, master, momentum):
    d = deltas.reshape(8, BLOCK, D)
    big = like((BLOCK, D), BF16)
    y = lax.axis_index("y")
    a = [lax.dynamic_index_in_dim(d, 4 + (y + s) % 4, keepdims=False) for s in range(4)]
    b = call(pack_rows, [big] * 4, d[:4])
    a = received(a, "y", FIRST)
    b = received(b, "x", FIRST)
    (base,) = call(early_base, [like((ROWS, D), F32)], master, momentum, after=[a[1]])
    base_other = swapped(base, "zhi", 1)

    outs = [like(SMALL, F32)] + [like(SMALL, BF16)] * 3
    total = [pltpu.VMEM((4, ROWS, D), F32)]
    sum_a = call(functools.partial(first_sum, "x"), outs, *a, scratch=total)
    sum_b = call(functools.partial(first_sum, "y"), outs, *b, scratch=total, after=[sum_a[0]])
    outs = [like(SMALL, BF16)]
    (own_a,) = call(second_sum, outs, *received(sum_a, "x", MIDDLE), after=[sum_b[0], base_other])
    (own_b,) = call(second_sum, outs, *received(sum_b, "y", MIDDLE), after=[own_a])
    other_a = swapped(own_a, "zhi", 1)
    other_b = swapped(own_b, "zhi", 1)
    (new_a,) = call(
        functools.partial(new_rows, 1), outs, own_a, other_a, base, base_other, after=[own_b],
    )
    (new_b,) = call(
        functools.partial(new_rows, 0), outs, own_b, other_b, base, base_other, after=[new_a],
    )
    all_a, all_b = call(
        join, [like(FOUR, BF16)] * 2,
        *received([new_a] * 4, "x", GATHER), *received([new_b] * 4, "y", GATHER),
    )
    master_out, momentum_out = call(
        new_state, [like((ROWS, D), F32)] * 2, own_a, other_a, own_b, other_b, base, momentum, after=[all_b],
    )
    a = received([all_a] * 4, "y", LAST)
    b = received([all_b] * 4, "x", LAST)
    whole = like((8, BLOCK, D), BF16)
    steps = (0,) + LAST

    def room(count):
        return [pltpu.VMEM((count, BLOCK, D), BF16), pltpu.SemaphoreType.DMA((count,))]

    (out,) = call(unpack_rows, [whole], *b, scratch=room(4), specs=([VMEM] * 4, [ANY]))
    for part in ((0, 1, 2), (3,)):
        n = len(part)
        (out,) = call(
            functools.partial(unpack_blocks, [steps[i] for i in part]), [whole], *[a[i] for i in part], out,
            scratch=room(n), aliases={n: 0}, specs=([VMEM] * n + [ANY], [ANY]),
        )
    return out.reshape(8 * BLOCK, D), master_out, momentum_out


def solution(mesh):
    parts = Mesh(mesh.devices.reshape(SIZES), AXES)
    rep = ("zhi", "y", "x")
    rows = P(("inner",) + rep, None)
    return jax.shard_map(
        local,
        mesh=parts,
        in_specs=(P(rep, "inner", None), rows, rows),
        out_specs=(P("inner", None), rows, rows),
        check_vma=False,
    )
```

time: 270 us -> 90.8 us (0.34)
  waiting for transfers between devices: 197 us -> 29.4 us
  starting transfers between devices: 13.3 us -> 52.9 us
  other arithmetic: 32.1 us -> 0 us
  between operations: 14.1 us -> 0.96 us
  local copies, waits for them, and re-layouts: 11.1 us -> 1.76 us
  Pallas kernels: 0 us -> 5.68 us
    convert_element_type x1 -> x0, waiting for transfers between devices: 106 us -> none  [reference(): weights_out = master_out.astype(jnp.bfloat16)]
    another operation x1 -> x0, waiting for transfers between devices: 91.7 us -> none
    ppermute x0 -> x27, starting transfers between devices: none -> 52.9 us  [moved(): return lax.ppermute(array, AXES, pairs)]
    add x32 -> x0, other arithmetic: 31.2 us -> none  [accumulate(): return running + deltas[index].astype(jnp.float32)]
    ppermute x0 -> x27, waiting for transfers between devices: none -> 29.4 us  [moved(): return lax.ppermute(array, AXES, pairs)]
    another operation x1 -> x0, starting transfers between devices: 13.3 us -> none
    pallas_call x0 -> x13, Pallas kernels: none -> 5.68 us  [call(): pl.pallas_call(kernel, out_shape=outs, in_specs=in_specs + [ANY] * len(af...]
    another operation x1 -> x0, local copies, waits for them, and re-layouts: 5.52 us -> none
  transfers between devices with their start and end apart: 2 -> 27, of which waited for: 2 -> 14; matrix products, arithmetic and copies ran while one was open for 0% -> 0% of each run, Pallas kernels for 0% -> 5%
where the time goes in v2:
time: 90.8 us; the launch traced here: 90.7 us
  starting transfers between devices  52.9 us (58%)
  waiting for transfers between devices  29.4 us (32%)
  Pallas kernels  5.68 us (6%)
  local copies, waits for them, and re-layouts  1.76 us (2%)
  between operations  0.96 us (1%)
    ppermute x27, starting transfers between devices, moved(): return lax.ppermute(array, AXES, pairs)  52.9 us
    ppermute x27, waiting for transfers between devices, moved(): return lax.ppermute(array, AXES, pairs)  29.4 us
    pallas_call x13, Pallas kernels, call(): pl.pallas_call(kernel, out_shape=outs, in_specs=in_specs + [ANY] * len(af...  5.68 us
  transfers between devices with their start and end apart: 27, of which 14 were waited for; matrix products, arithmetic and copies ran while one was open for 0% of the time, Pallas kernels for 5%

profile of v2, /device:TPU:32, one launch (start us, length us, event | category | flops | bytes accessed | tf_op | source)
XLA Modules:
  0.0 90.7 jit_solution(1423076342194879100)
XLA Ops:
  0.7 1.6 %dynamic-slice_bitcast_fusion = (bf16[80,2560]{1,0:T(8,128)(2,1)S(1)}, bf16[80,2560]{1,0:T(8,128)(2,1)S(1)}, bf16[80,2560]{1,0:T(8,128)(2,1)S(1)}, bf16[80,2560]{1,0:T(8,128)(2,1)S(1)}) fusion(bf16[8,80,2560]{2,1,0:T(8,128)(2,1)} %bitcast.13, s32[]{:T(128)S(6)} %select_n.39, s32[]{:T(128)S(6)} %select_n.37, s32[]{:T(128)S(6)} %select_n.35, s32[]{:T(128)S(6)} %select_n.33), kind=kLoop, calls=%fused_computation | loop fusion | bytes 3276816 | tf_op jit(solution)/shard_map/jit(dynamic_index_in_dim)/squeeze | solution.py:184
  2.3 1.7 %collective-permute-start = (bf16[80,2560]{1,0:T(8,128)(2,1)S(1)}, bf16[80,2560]{1,0:T(8,128)(2,1)S(1)}, u32[]{:S(2)}, u32[]{:S(2)}) collective-permute-start(bf16[80,2560]{1,0:T(8,128)(2,1)S(1)} %get-tuple-element.37), channel_id=1, source_target_pairs={{0,32},{1,33},{2,34},{3,35},{4,36},{5,37},{6,38},{7,39},{8,40},{9,... | collective-permute-start | bytes 1228808 | tf_op jit(solution)/shard_map/ppermute | solution.py:42
  4.0 1.7 %collective-permute-start.1 = (bf16[80,2560]{1,0:T(8,128)(2,1)S(1)}, bf16[80,2560]{1,0:T(8,128)(2,1)S(1)}, u32[]{:S(2)}, u32[]{:S(2)}) collective-permute-start(bf16[80,2560]{1,0:T(8,128)(2,1)S(1)} %get-tuple-element.36), channel_id=1, source_target_pairs={{0,96},{1,97},{2,98},{3,99},{4,100},{5,101},{6,102},{7,103},{8,104... | collective-permute-start | bytes 1228808 | tf_op jit(solution)/shard_map/ppermute | solution.py:42
  5.7 2.0 %collective-permute-start.2 = (bf16[80,2560]{1,0:T(8,128)(2,1)S(1)}, bf16[80,2560]{1,0:T(8,128)(2,1)S(1)}, u32[]{:S(2)}, u32[]{:S(2)}) collective-permute-start(bf16[80,2560]{1,0:T(8,128)(2,1)S(1)} %get-tuple-element.35), channel_id=1, source_target_pairs={{0,64},{1,65},{2,66},{3,67},{4,68},{5,69},{6,70},{7,71},{8,72},{9,... | collective-permute-start | bytes 1228808 | tf_op jit(solution)/shard_map/ppermute | solution.py:42
  8.0 1.6 %collective-permute-start.6 = (bf16[80,2560]{1,0:T(8,128)(2,1)S(1)}, bf16[80,2560]{1,0:T(8,128)(2,1)S(1)}, u32[]{:S(2)}, u32[]{:S(2)}) collective-permute-start(bf16[80,2560]{1,0:T(8,128)(2,1)S(1)} %get-tuple-element.24), channel_id=1, source_target_pairs={{0,8},{1,9},{2,10},{3,11},{4,12},{5,13},{6,14},{7,15},{8,16},{9,17... | collective-permute-start | bytes 1228808 | tf_op jit(solution)/shard_map/ppermute | solution.py:42
  9.6 1.7 %collective-permute-start.7 = (bf16[80,2560]{1,0:T(8,128)(2,1)S(1)}, bf16[80,2560]{1,0:T(8,128)(2,1)S(1)}, u32[]{:S(2)}, u32[]{:S(2)}) collective-permute-start(bf16[80,2560]{1,0:T(8,128)(2,1)S(1)} %get-tuple-element.25), channel_id=1, source_target_pairs={{0,24},{1,25},{2,26},{3,27},{4,28},{5,29},{6,30},{7,31},{8,0},{9,1... | collective-permute-start | bytes 1228808 | tf_op jit(solution)/shard_map/ppermute | solution.py:42
  11.3 3.6 %collective-permute-done.refs_1_.refs_2_ = bf16[80,2560]{1,0:T(8,128)(2,1)S(1)} collective-permute-done((bf16[80,2560]{1,0:T(8,128)(2,1)S(1)}, bf16[80,2560]{1,0:T(8,128)(2,1)S(1)}, u32[]{:S(2)}, u32[]{:S(2)}) %collective-permute-start) | collective-permute-done | bytes 409632 | tf_op jit(solution)/shard_map/ppermute | solution.py:42
  14.9 3.0 %collective-permute-start.8 = (bf16[80,2560]{1,0:T(8,128)(2,1)S(1)}, bf16[80,2560]{1,0:T(8,128)(2,1)S(1)}, u32[]{:S(2)}, u32[]{:S(2)}) collective-permute-start(bf16[80,2560]{1,0:T(8,128)(2,1)S(1)} %get-tuple-element.26), channel_id=1, source_target_pairs={{0,16},{1,17},{2,18},{3,19},{4,20},{5,21},{6,22},{7,23},{8,24},{9,... | collective-permute-start | bytes 1228808 | tf_op jit(solution)/shard_map/ppermute | solution.py:42
  18.0 5.1 %collective-permute-done.1.refs_2_ = bf16[80,2560]{1,0:T(8,128)(2,1)S(1)} collective-permute-done((bf16[80,2560]{1,0:T(8,128)(2,1)S(1)}, bf16[80,2560]{1,0:T(8,128)(2,1)S(1)}, u32[]{:S(2)}, u32[]{:S(2)}) %collective-permute-start.1) | collective-permute-done | bytes 409632 | tf_op jit(solution)/shard_map/ppermute | solution.py:42
  23.1 6.3 %collective-permute-start.9 = (f32[20,2560]{1,0:T(8,128)S(1)}, f32[20,2560]{1,0:T(8,128)S(1)}, u32[]{:S(2)}, u32[]{:S(2)}) collective-permute-start(f32[20,2560]{1,0:T(8,128)S(1)} %shard_map.61.refs_2_.refs_4_), channel_id=1, source_target_pairs={{0,128},{1,129},{2,130},{3,131},{4,132},{5,133},{6,134},{7,135},{8... | collective-permute-start | bytes 614408 | tf_op jit(solution)/shard_map/ppermute | solution.py:42
  29.8 1.6 %collective-permute-start.3 = (bf16[40,1280]{1,0:T(8,128)(2,1)S(1)}, bf16[40,1280]{1,0:T(8,128)(2,1)S(1)}, u32[]{:S(2)}, u32[]{:S(2)}) collective-permute-start(bf16[40,1280]{1,0:T(8,128)(2,1)S(1)} %get-tuple-element.20), channel_id=1, source_target_pairs={{0,8},{1,9},{2,10},{3,11},{4,12},{5,13},{6,14},{7,15},{8,16},{9,17... | collective-permute-start | bytes 307208 | tf_op jit(solution)/shard_map/ppermute | solution.py:42
  31.3 1.7 %collective-permute-start.4 = (bf16[40,1280]{1,0:T(8,128)(2,1)S(1)}, bf16[40,1280]{1,0:T(8,128)(2,1)S(1)}, u32[]{:S(2)}, u32[]{:S(2)}) collective-permute-start(bf16[40,1280]{1,0:T(8,128)(2,1)S(1)} %get-tuple-element.21), channel_id=1, source_target_pairs={{0,24},{1,25},{2,26},{3,27},{4,28},{5,29},{6,30},{7,31},{8,0},{9,1... | collective-permute-start | bytes 307208 | tf_op jit(solution)/shard_map/ppermute | solution.py:42
  33.1 1.8 %collective-permute-start.5 = (bf16[40,1280]{1,0:T(8,128)(2,1)S(1)}, bf16[40,1280]{1,0:T(8,128)(2,1)S(1)}, u32[]{:S(2)}, u32[]{:S(2)}) collective-permute-start(bf16[40,1280]{1,0:T(8,128)(2,1)S(1)} %get-tuple-element.22), channel_id=1, source_target_pairs={{0,16},{1,17},{2,18},{3,19},{4,20},{5,21},{6,22},{7,23},{8,24},{9,... | collective-permute-start | bytes 307208 | tf_op jit(solution)/shard_map/ppermute | solution.py:42
  35.7 3.7 %collective-permute-start.12 = (bf16[40,1280]{1,0:T(8,128)(2,1)S(1)}, bf16[40,1280]{1,0:T(8,128)(2,1)S(1)}, u32[]{:S(2)}, u32[]{:S(2)}) collective-permute-start(bf16[40,1280]{1,0:T(8,128)(2,1)S(1)} %get-tuple-element.29), channel_id=1, source_target_pairs={{0,96},{1,97},{2,98},{3,99},{4,100},{5,101},{6,102},{7,103},{8,104... | collective-permute-start | bytes 307208 | tf_op jit(solution)/shard_map/ppermute | solution.py:42
  39.4 2.7 %collective-permute-start.13 = (bf16[40,1280]{1,0:T(8,128)(2,1)S(1)}, bf16[40,1280]{1,0:T(8,128)(2,1)S(1)}, u32[]{:S(2)}, u32[]{:S(2)}) collective-permute-start(bf16[40,1280]{1,0:T(8,128)(2,1)S(1)} %get-tuple-element.30), channel_id=1, source_target_pairs={{0,64},{1,65},{2,66},{3,67},{4,68},{5,69},{6,70},{7,71},{8,72},{9,... | collective-permute-start | bytes 307208 | tf_op jit(solution)/shard_map/ppermute | solution.py:42
  42.2 3.3 %collective-permute-start.10 = (bf16[40,1280]{1,0:T(8,128)(2,1)S(1)}, bf16[40,1280]{1,0:T(8,128)(2,1)S(1)}, u32[]{:S(2)}, u32[]{:S(2)}) collective-permute-start(bf16[40,1280]{1,0:T(8,128)(2,1)S(1)} %shard_map.62.refs_4_.refs_0_), channel_id=1, source_target_pairs={{0,128},{1,129},{2,130},{3,131},{4,132},{5,133},{6,134},{7,135},{8... | collective-permute-start | bytes 307208 | tf_op jit(solution)/shard_map/ppermute | solution.py:42
  45.6 2.9 %collective-permute-start.17 = (bf16[40,1280]{1,0:T(8,128)(2,1)S(1)}, bf16[40,1280]{1,0:T(8,128)(2,1)S(1)}, u32[]{:S(2)}, u32[]{:S(2)}) collective-permute-start(bf16[40,1280]{1,0:T(8,128)(2,1)S(1)} %shard_map.63.refs_4_.refs_0_.refs_2_), channel_id=1, source_target_pairs={{0,128},{1,129},{2,130},{3,131},{4,132},{5,133},{6,134},{7,135},{8... | collective-permute-start | bytes 307208 | tf_op jit(solution)/shard_map/ppermute | solution.py:42
  48.5 3.5 %collective-permute-done.10.refs_1_ = bf16[40,1280]{1,0:T(8,128)(2,1)S(1)} collective-permute-done((bf16[40,1280]{1,0:T(8,128)(2,1)S(1)}, bf16[40,1280]{1,0:T(8,128)(2,1)S(1)}, u32[]{:S(2)}, u32[]{:S(2)}) %collective-permute-start.10) | collective-permute-done | bytes 102432 | tf_op jit(solution)/shard_map/ppermute | solution.py:42
  52.1 2.6 %collective-permute-done.17.refs_1_.refs_3_ = bf16[40,1280]{1,0:T(8,128)(2,1)S(1)} collective-permute-done((bf16[40,1280]{1,0:T(8,128)(2,1)S(1)}, bf16[40,1280]{1,0:T(8,128)(2,1)S(1)}, u32[]{:S(2)}, u32[]{:S(2)}) %collective-permute-start.17) | collective-permute-done | bytes 102432 | tf_op jit(solution)/shard_map/ppermute | solution.py:42
  54.8 2.5 %collective-permute-start.18 = (bf16[40,1280]{1,0:T(8,128)(2,1)S(1)}, bf16[40,1280]{1,0:T(8,128)(2,1)S(1)}, u32[]{:S(2)}, u32[]{:S(2)}) collective-permute-start(bf16[40,1280]{1,0:T(8,128)(2,1)S(1)} %shard_map.65.refs_4_), channel_id=1, source_target_pairs={{0,64},{1,65},{2,66},{3,67},{4,68},{5,69},{6,70},{7,71},{8,72},{9,... | collective-permute-start | bytes 307208 | tf_op jit(solution)/shard_map/ppermute | solution.py:42
  57.4 2.1 %collective-permute-start.19 = (bf16[40,1280]{1,0:T(8,128)(2,1)S(1)}, bf16[40,1280]{1,0:T(8,128)(2,1)S(1)}, u32[]{:S(2)}, u32[]{:S(2)}) collective-permute-start(bf16[40,1280]{1,0:T(8,128)(2,1)S(1)} %shard_map.65.refs_4_), channel_id=1, source_target_pairs={{0,96},{1,97},{2,98},{3,99},{4,100},{5,101},{6,102},{7,103},{8,104... | collective-permute-start | bytes 307208 | tf_op jit(solution)/shard_map/ppermute | solution.py:42
  59.4 3.8 %collective-permute-start.14 = (bf16[40,1280]{1,0:T(8,128)(2,1)S(1)}, bf16[40,1280]{1,0:T(8,128)(2,1)S(1)}, u32[]{:S(2)}, u32[]{:S(2)}) collective-permute-start(bf16[40,1280]{1,0:T(8,128)(2,1)S(1)} %shard_map.64.refs_4_.refs_0_), channel_id=1, source_target_pairs={{0,16},{1,17},{2,18},{3,19},{4,20},{5,21},{6,22},{7,23},{8,24},{9,... | collective-permute-start | bytes 307208 | tf_op jit(solution)/shard_map/ppermute | solution.py:42
  63.6 1.6 %collective-permute-start.16 = (bf16[40,1280]{1,0:T(8,128)(2,1)S(1)}, bf16[40,1280]{1,0:T(8,128)(2,1)S(1)}, u32[]{:S(2)}, u32[]{:S(2)}) collective-permute-start(bf16[40,1280]{1,0:T(8,128)(2,1)S(1)} %shard_map.64.refs_4_.refs_0_), channel_id=1, source_target_pairs={{0,8},{1,9},{2,10},{3,11},{4,12},{5,13},{6,14},{7,15},{8,16},{9,17... | collective-permute-start | bytes 307208 | tf_op jit(solution)/shard_map/ppermute | solution.py:42
  65.3 4.4 %collective-permute-done.20.refs_7_ = bf16[40,1280]{1,0:T(8,128)(2,1)S(1)} collective-permute-done((bf16[40,1280]{1,0:T(8,128)(2,1)S(1)}, bf16[40,1280]{1,0:T(8,128)(2,1)S(1)}, u32[]{:S(2)}, u32[]{:S(2)}) %collective-permute-start.20) | collective-permute-done | bytes 102432 | tf_op jit(solution)/shard_map/ppermute | solution.py:42
  70.9 1.9 %collective-permute-start.24 = (bf16[4,40,1280]{2,1,0:T(8,128)(2,1)S(1)}, bf16[4,40,1280]{2,1,0:T(8,128)(2,1)S(1)}, u32[]{:S(2)}, u32[]{:S(2)}) collective-permute-start(bf16[4,40,1280]{2,1,0:T(8,128)(2,1)S(1)} %get-tuple-element.32.refs_0_.refs_6_), channel_id=1, source_target_pairs={{0,16},{1,17},{2,18},{3,19},{4,20},{5,21},{6,22},{7,23},{8,24},{9,... | collective-permute-start | bytes 1228808 | tf_op jit(solution)/shard_map/ppermute | solution.py:42
  72.7 1.3 %collective-permute-start.25 = (bf16[4,40,1280]{2,1,0:T(8,128)(2,1)S(1)}, bf16[4,40,1280]{2,1,0:T(8,128)(2,1)S(1)}, u32[]{:S(2)}, u32[]{:S(2)}) collective-permute-start(bf16[4,40,1280]{2,1,0:T(8,128)(2,1)S(1)} %get-tuple-element.32.refs_0_.refs_6_), channel_id=1, source_target_pairs={{0,24},{1,25},{2,26},{3,27},{4,28},{5,29},{6,30},{7,31},{8,0},{9,1... | collective-permute-start | bytes 1228808 | tf_op jit(solution)/shard_map/ppermute | solution.py:42
  75.5 1.9 %collective-permute-start.23 = (bf16[4,40,1280]{2,1,0:T(8,128)(2,1)S(1)}, bf16[4,40,1280]{2,1,0:T(8,128)(2,1)S(1)}, u32[]{:S(2)}, u32[]{:S(2)}) collective-permute-start(bf16[4,40,1280]{2,1,0:T(8,128)(2,1)S(1)} %get-tuple-element.31.refs_0_), channel_id=1, source_target_pairs={{0,96},{1,97},{2,98},{3,99},{4,100},{5,101},{6,102},{7,103},{8,104... | collective-permute-start | bytes 1228808 | tf_op jit(solution)/shard_map/ppermute | solution.py:42
  77.4 3.1 %collective-permute-done.24.refs_1_ = bf16[4,40,1280]{2,1,0:T(8,128)(2,1)S(1)} collective-permute-done((bf16[4,40,1280]{2,1,0:T(8,128)(2,1)S(1)}, bf16[4,40,1280]{2,1,0:T(8,128)(2,1)S(1)}, u32[]{:S(2)}, u32[]{:S(2)}) %collective-permute-start.24) | collective-permute-done | bytes 409632 | tf_op jit(solution)/shard_map/ppermute | solution.py:42
  81.6 1.5 %collective-permute-done.25.refs_2_ = bf16[4,40,1280]{2,1,0:T(8,128)(2,1)S(1)} collective-permute-done((bf16[4,40,1280]{2,1,0:T(8,128)(2,1)S(1)}, bf16[4,40,1280]{2,1,0:T(8,128)(2,1)S(1)}, u32[]{:S(2)}, u32[]{:S(2)}) %collective-permute-start.25) | collective-permute-done | bytes 409632 | tf_op jit(solution)/shard_map/ppermute | solution.py:42
  83.1 1.7 %collective-permute-done.26.refs_3_ = bf16[4,40,1280]{2,1,0:T(8,128)(2,1)S(1)} collective-permute-done((bf16[4,40,1280]{2,1,0:T(8,128)(2,1)S(1)}, bf16[4,40,1280]{2,1,0:T(8,128)(2,1)S(1)}, u32[]{:S(2)}, u32[]{:S(2)}) %collective-permute-start.26) | collective-permute-done | bytes 409632 | tf_op jit(solution)/shard_map/ppermute | solution.py:42
  84.8 1.3 %shard_map.67.refs_3_ = bf16[8,80,2560]{2,1,0:T(8,128)(2,1)} custom-call(bf16[4,40,1280]{2,1,0:T(8,128)(2,1)S(1)} %get-tuple-element.32.refs_0_.refs_6_, bf16[4,40,1280]{2,1,0:T(8,128)(2,1)S(1)} %collective-permute-done.24.refs_1_, bf16[4,40,1280]{2,1,0:T(8,128)(2,1)S(1)} %collective-permute-done.25.refs_2_, ...), custom_call_target="tpu_custom_call" | custom-call | flops 4915200 | bytes 4915200 | tf_op jit(solution)/shard_map/pallas_call | solution.py:66
  86.1 1.4 %collective-permute-done.23.refs_2_ = bf16[4,40,1280]{2,1,0:T(8,128)(2,1)S(1)} collective-permute-done((bf16[4,40,1280]{2,1,0:T(8,128)(2,1)S(1)}, bf16[4,40,1280]{2,1,0:T(8,128)(2,1)S(1)}, u32[]{:S(2)}, u32[]{:S(2)}) %collective-permute-start.23) | collective-permute-done | bytes 409632 | tf_op jit(solution)/shard_map/ppermute | solution.py:42
  (43 shorter events, 9.2 us)
Async XLA Ops:
  0.6 7.0 %copy-start.2 = (bf16[1,640,2560]{2,1,0:T(8,128)(2,1)S(1)}, bf16[1,640,2560]{2,1,0:T(8,128)(2,1)}, u32[]{:S(2)}) copy-start(bf16[1,640,2560]{2,1,0:T(8,128)(2,1)} %param.3) | copy-start | bytes 9830404
  2.3 15.6 %copy-start = (f32[20,2560]{1,0:T(8,128)S(1)}, f32[20,2560]{1,0:T(8,128)}, u32[]{:S(2)}) copy-start(f32[20,2560]{1,0:T(8,128)} %refs_5_.1) | copy-start | bytes 614404
  2.3 15.6 %copy-start.1 = (f32[20,2560]{1,0:T(8,128)S(1)}, f32[20,2560]{1,0:T(8,128)}, u32[]{:S(2)}) copy-start(f32[20,2560]{1,0:T(8,128)} %refs_0_.1) | copy-start | bytes 614404
  2.3 12.6 %collective-permute-start = (bf16[80,2560]{1,0:T(8,128)(2,1)S(1)}, bf16[80,2560]{1,0:T(8,128)(2,1)S(1)}, u32[]{:S(2)}, u32[]{:S(2)}) collective-permute-start(bf16[80,2560]{1,0:T(8,128)(2,1)S(1)} %get-tuple-element.37), channel_id=1, source_target_pairs={{0,32},{1,33},{2,34},{3,35},{4,36},{5,37},{6,38},{7,39},{8,40},{9,... | collective-permute-start | bytes 1228808 | tf_op jit(solution)/shard_map/ppermute | solution.py:42
  4.0 19.1 %collective-permute-start.1 = (bf16[80,2560]{1,0:T(8,128)(2,1)S(1)}, bf16[80,2560]{1,0:T(8,128)(2,1)S(1)}, u32[]{:S(2)}, u32[]{:S(2)}) collective-permute-start(bf16[80,2560]{1,0:T(8,128)(2,1)S(1)} %get-tuple-element.36), channel_id=1, source_target_pairs={{0,96},{1,97},{2,98},{3,99},{4,100},{5,101},{6,102},{7,103},{8,104... | collective-permute-start | bytes 1228808 | tf_op jit(solution)/shard_map/ppermute | solution.py:42
  5.7 23.7 %collective-permute-start.2 = (bf16[80,2560]{1,0:T(8,128)(2,1)S(1)}, bf16[80,2560]{1,0:T(8,128)(2,1)S(1)}, u32[]{:S(2)}, u32[]{:S(2)}) collective-permute-start(bf16[80,2560]{1,0:T(8,128)(2,1)S(1)} %get-tuple-element.35), channel_id=1, source_target_pairs={{0,64},{1,65},{2,66},{3,67},{4,68},{5,69},{6,70},{7,71},{8,72},{9,... | collective-permute-start | bytes 1228808 | tf_op jit(solution)/shard_map/ppermute | solution.py:42
  8.0 23.3 %collective-permute-start.6 = (bf16[80,2560]{1,0:T(8,128)(2,1)S(1)}, bf16[80,2560]{1,0:T(8,128)(2,1)S(1)}, u32[]{:S(2)}, u32[]{:S(2)}) collective-permute-start(bf16[80,2560]{1,0:T(8,128)(2,1)S(1)} %get-tuple-element.24), channel_id=1, source_target_pairs={{0,8},{1,9},{2,10},{3,11},{4,12},{5,13},{6,14},{7,15},{8,16},{9,17... | collective-permute-start | bytes 1228808 | tf_op jit(solution)/shard_map/ppermute | solution.py:42
  9.6 23.5 %collective-permute-start.7 = (bf16[80,2560]{1,0:T(8,128)(2,1)S(1)}, bf16[80,2560]{1,0:T(8,128)(2,1)S(1)}, u32[]{:S(2)}, u32[]{:S(2)}) collective-permute-start(bf16[80,2560]{1,0:T(8,128)(2,1)S(1)} %get-tuple-element.25), channel_id=1, source_target_pairs={{0,24},{1,25},{2,26},{3,27},{4,28},{5,29},{6,30},{7,31},{8,0},{9,1... | collective-permute-start | bytes 1228808 | tf_op jit(solution)/shard_map/ppermute | solution.py:42
  14.9 20.0 %collective-permute-start.8 = (bf16[80,2560]{1,0:T(8,128)(2,1)S(1)}, bf16[80,2560]{1,0:T(8,128)(2,1)S(1)}, u32[]{:S(2)}, u32[]{:S(2)}) collective-permute-start(bf16[80,2560]{1,0:T(8,128)(2,1)S(1)} %get-tuple-element.26), channel_id=1, source_target_pairs={{0,16},{1,17},{2,18},{3,19},{4,20},{5,21},{6,22},{7,23},{8,24},{9,... | collective-permute-start | bytes 1228808 | tf_op jit(solution)/shard_map/ppermute | solution.py:42
  23.1 19.1 %collective-permute-start.9 = (f32[20,2560]{1,0:T(8,128)S(1)}, f32[20,2560]{1,0:T(8,128)S(1)}, u32[]{:S(2)}, u32[]{:S(2)}) collective-permute-start(f32[20,2560]{1,0:T(8,128)S(1)} %shard_map.61.refs_2_.refs_4_), channel_id=1, source_target_pairs={{0,128},{1,129},{2,130},{3,131},{4,132},{5,133},{6,134},{7,135},{8... | collective-permute-start | bytes 614408 | tf_op jit(solution)/shard_map/ppermute | solution.py:42
  29.8 5.9 %collective-permute-start.3 = (bf16[40,1280]{1,0:T(8,128)(2,1)S(1)}, bf16[40,1280]{1,0:T(8,128)(2,1)S(1)}, u32[]{:S(2)}, u32[]{:S(2)}) collective-permute-start(bf16[40,1280]{1,0:T(8,128)(2,1)S(1)} %get-tuple-element.20), channel_id=1, source_target_pairs={{0,8},{1,9},{2,10},{3,11},{4,12},{5,13},{6,14},{7,15},{8,16},{9,17... | collective-permute-start | bytes 307208 | tf_op jit(solution)/shard_map/ppermute | solution.py:42
  31.3 8.0 %collective-permute-start.4 = (bf16[40,1280]{1,0:T(8,128)(2,1)S(1)}, bf16[40,1280]{1,0:T(8,128)(2,1)S(1)}, u32[]{:S(2)}, u32[]{:S(2)}) collective-permute-start(bf16[40,1280]{1,0:T(8,128)(2,1)S(1)} %get-tuple-element.21), channel_id=1, source_target_pairs={{0,24},{1,25},{2,26},{3,27},{4,28},{5,29},{6,30},{7,31},{8,0},{9,1... | collective-permute-start | bytes 307208 | tf_op jit(solution)/shard_map/ppermute | solution.py:42
  33.1 9.0 %collective-permute-start.5 = (bf16[40,1280]{1,0:T(8,128)(2,1)S(1)}, bf16[40,1280]{1,0:T(8,128)(2,1)S(1)}, u32[]{:S(2)}, u32[]{:S(2)}) collective-permute-start(bf16[40,1280]{1,0:T(8,128)(2,1)S(1)} %get-tuple-element.22), channel_id=1, source_target_pairs={{0,16},{1,17},{2,18},{3,19},{4,20},{5,21},{6,22},{7,23},{8,24},{9,... | collective-permute-start | bytes 307208 | tf_op jit(solution)/shard_map/ppermute | solution.py:42
  35.3 10.1 %collective-permute-start.11 = (bf16[40,1280]{1,0:T(8,128)(2,1)S(1)}, bf16[40,1280]{1,0:T(8,128)(2,1)S(1)}, u32[]{:S(2)}, u32[]{:S(2)}) collective-permute-start(bf16[40,1280]{1,0:T(8,128)(2,1)S(1)} %get-tuple-element.28), channel_id=1, source_target_pairs={{0,32},{1,33},{2,34},{3,35},{4,36},{5,37},{6,38},{7,39},{8,40},{9,... | collective-permute-start | bytes 307208 | tf_op jit(solution)/shard_map/ppermute | solution.py:42
  35.7 9.7 %collective-permute-start.12 = (bf16[40,1280]{1,0:T(8,128)(2,1)S(1)}, bf16[40,1280]{1,0:T(8,128)(2,1)S(1)}, u32[]{:S(2)}, u32[]{:S(2)}) collective-permute-start(bf16[40,1280]{1,0:T(8,128)(2,1)S(1)} %get-tuple-element.29), channel_id=1, source_target_pairs={{0,96},{1,97},{2,98},{3,99},{4,100},{5,101},{6,102},{7,103},{8,104... | collective-permute-start | bytes 307208 | tf_op jit(solution)/shard_map/ppermute | solution.py:42
  39.4 6.2 %collective-permute-start.13 = (bf16[40,1280]{1,0:T(8,128)(2,1)S(1)}, bf16[40,1280]{1,0:T(8,128)(2,1)S(1)}, u32[]{:S(2)}, u32[]{:S(2)}) collective-permute-start(bf16[40,1280]{1,0:T(8,128)(2,1)S(1)} %get-tuple-element.30), channel_id=1, source_target_pairs={{0,64},{1,65},{2,66},{3,67},{4,68},{5,69},{6,70},{7,71},{8,72},{9,... | collective-permute-start | bytes 307208 | tf_op jit(solution)/shard_map/ppermute | solution.py:42
  42.2 9.9 %collective-permute-start.10 = (bf16[40,1280]{1,0:T(8,128)(2,1)S(1)}, bf16[40,1280]{1,0:T(8,128)(2,1)S(1)}, u32[]{:S(2)}, u32[]{:S(2)}) collective-permute-start(bf16[40,1280]{1,0:T(8,128)(2,1)S(1)} %shard_map.62.refs_4_.refs_0_), channel_id=1, source_target_pairs={{0,128},{1,129},{2,130},{3,131},{4,132},{5,133},{6,134},{7,135},{8... | collective-permute-start | bytes 307208 | tf_op jit(solution)/shard_map/ppermute | solution.py:42
  45.6 9.1 %collective-permute-start.17 = (bf16[40,1280]{1,0:T(8,128)(2,1)S(1)}, bf16[40,1280]{1,0:T(8,128)(2,1)S(1)}, u32[]{:S(2)}, u32[]{:S(2)}) collective-permute-start(bf16[40,1280]{1,0:T(8,128)(2,1)S(1)} %shard_map.63.refs_4_.refs_0_.refs_2_), channel_id=1, source_target_pairs={{0,128},{1,129},{2,130},{3,131},{4,132},{5,133},{6,134},{7,135},{8... | collective-permute-start | bytes 307208 | tf_op jit(solution)/shard_map/ppermute | solution.py:42
  54.8 8.8 %collective-permute-start.18 = (bf16[40,1280]{1,0:T(8,128)(2,1)S(1)}, bf16[40,1280]{1,0:T(8,128)(2,1)S(1)}, u32[]{:S(2)}, u32[]{:S(2)}) collective-permute-start(bf16[40,1280]{1,0:T(8,128)(2,1)S(1)} %shard_map.65.refs_4_), channel_id=1, source_target_pairs={{0,64},{1,65},{2,66},{3,67},{4,68},{5,69},{6,70},{7,71},{8,72},{9,... | collective-permute-start | bytes 307208 | tf_op jit(solution)/shard_map/ppermute | solution.py:42
  57.4 7.9 %collective-permute-start.19 = (bf16[40,1280]{1,0:T(8,128)(2,1)S(1)}, bf16[40,1280]{1,0:T(8,128)(2,1)S(1)}, u32[]{:S(2)}, u32[]{:S(2)}) collective-permute-start(bf16[40,1280]{1,0:T(8,128)(2,1)S(1)} %shard_map.65.refs_4_), channel_id=1, source_target_pairs={{0,96},{1,97},{2,98},{3,99},{4,100},{5,101},{6,102},{7,103},{8,104... | collective-permute-start | bytes 307208 | tf_op jit(solution)/shard_map/ppermute | solution.py:42
  59.4 10.3 %collective-permute-start.20 = (bf16[40,1280]{1,0:T(8,128)(2,1)S(1)}, bf16[40,1280]{1,0:T(8,128)(2,1)S(1)}, u32[]{:S(2)}, u32[]{:S(2)}) collective-permute-start(bf16[40,1280]{1,0:T(8,128)(2,1)S(1)} %shard_map.65.refs_4_), channel_id=1, source_target_pairs={{0,32},{1,33},{2,34},{3,35},{4,36},{5,37},{6,38},{7,39},{8,40},{9,... | collective-permute-start | bytes 307208 | tf_op jit(solution)/shard_map/ppermute | solution.py:42
  59.4 10.3 %collective-permute-start.14 = (bf16[40,1280]{1,0:T(8,128)(2,1)S(1)}, bf16[40,1280]{1,0:T(8,128)(2,1)S(1)}, u32[]{:S(2)}, u32[]{:S(2)}) collective-permute-start(bf16[40,1280]{1,0:T(8,128)(2,1)S(1)} %shard_map.64.refs_4_.refs_0_), channel_id=1, source_target_pairs={{0,16},{1,17},{2,18},{3,19},{4,20},{5,21},{6,22},{7,23},{8,24},{9,... | collective-permute-start | bytes 307208 | tf_op jit(solution)/shard_map/ppermute | solution.py:42
  63.2 7.2 %collective-permute-start.15 = (bf16[40,1280]{1,0:T(8,128)(2,1)S(1)}, bf16[40,1280]{1,0:T(8,128)(2,1)S(1)}, u32[]{:S(2)}, u32[]{:S(2)}) collective-permute-start(bf16[40,1280]{1,0:T(8,128)(2,1)S(1)} %shard_map.64.refs_4_.refs_0_), channel_id=1, source_target_pairs={{0,24},{1,25},{2,26},{3,27},{4,28},{5,29},{6,30},{7,31},{8,0},{9,1... | collective-permute-start | bytes 307208 | tf_op jit(solution)/shard_map/ppermute | solution.py:42
  63.6 7.2 %collective-permute-start.16 = (bf16[40,1280]{1,0:T(8,128)(2,1)S(1)}, bf16[40,1280]{1,0:T(8,128)(2,1)S(1)}, u32[]{:S(2)}, u32[]{:S(2)}) collective-permute-start(bf16[40,1280]{1,0:T(8,128)(2,1)S(1)} %shard_map.64.refs_4_.refs_0_), channel_id=1, source_target_pairs={{0,8},{1,9},{2,10},{3,11},{4,12},{5,13},{6,14},{7,15},{8,16},{9,17... | collective-permute-start | bytes 307208 | tf_op jit(solution)/shard_map/ppermute | solution.py:42
  70.9 9.6 %collective-permute-start.24 = (bf16[4,40,1280]{2,1,0:T(8,128)(2,1)S(1)}, bf16[4,40,1280]{2,1,0:T(8,128)(2,1)S(1)}, u32[]{:S(2)}, u32[]{:S(2)}) collective-permute-start(bf16[4,40,1280]{2,1,0:T(8,128)(2,1)S(1)} %get-tuple-element.32.refs_0_.refs_6_), channel_id=1, source_target_pairs={{0,16},{1,17},{2,18},{3,19},{4,20},{5,21},{6,22},{7,23},{8,24},{9,... | collective-permute-start | bytes 1228808 | tf_op jit(solution)/shard_map/ppermute | solution.py:42
  72.7 10.4 %collective-permute-start.25 = (bf16[4,40,1280]{2,1,0:T(8,128)(2,1)S(1)}, bf16[4,40,1280]{2,1,0:T(8,128)(2,1)S(1)}, u32[]{:S(2)}, u32[]{:S(2)}) collective-permute-start(bf16[4,40,1280]{2,1,0:T(8,128)(2,1)S(1)} %get-tuple-element.32.refs_0_.refs_6_), channel_id=1, source_target_pairs={{0,24},{1,25},{2,26},{3,27},{4,28},{5,29},{6,30},{7,31},{8,0},{9,1... | collective-permute-start | bytes 1228808 | tf_op jit(solution)/shard_map/ppermute | solution.py:42
  74.0 10.7 %collective-permute-start.26 = (bf16[4,40,1280]{2,1,0:T(8,128)(2,1)S(1)}, bf16[4,40,1280]{2,1,0:T(8,128)(2,1)S(1)}, u32[]{:S(2)}, u32[]{:S(2)}) collective-permute-start(bf16[4,40,1280]{2,1,0:T(8,128)(2,1)S(1)} %get-tuple-element.32.refs_0_.refs_6_), channel_id=1, source_target_pairs={{0,8},{1,9},{2,10},{3,11},{4,12},{5,13},{6,14},{7,15},{8,16},{9,17... | collective-permute-start | bytes 1228808 | tf_op jit(solution)/shard_map/ppermute | solution.py:42
  74.8 11.4 %collective-permute-start.22 = (bf16[4,40,1280]{2,1,0:T(8,128)(2,1)S(1)}, bf16[4,40,1280]{2,1,0:T(8,128)(2,1)S(1)}, u32[]{:S(2)}, u32[]{:S(2)}) collective-permute-start(bf16[4,40,1280]{2,1,0:T(8,128)(2,1)S(1)} %get-tuple-element.31.refs_0_), channel_id=1, source_target_pairs={{0,64},{1,65},{2,66},{3,67},{4,68},{5,69},{6,70},{7,71},{8,72},{9,... | collective-permute-start | bytes 1228808 | tf_op jit(solution)/shard_map/ppermute | solution.py:42
  75.5 12.0 %collective-permute-start.23 = (bf16[4,40,1280]{2,1,0:T(8,128)(2,1)S(1)}, bf16[4,40,1280]{2,1,0:T(8,128)(2,1)S(1)}, u32[]{:S(2)}, u32[]{:S(2)}) collective-permute-start(bf16[4,40,1280]{2,1,0:T(8,128)(2,1)S(1)} %get-tuple-element.31.refs_0_), channel_id=1, source_target_pairs={{0,96},{1,97},{2,98},{3,99},{4,100},{5,101},{6,102},{7,103},{8,104... | collective-permute-start | bytes 1228808 | tf_op jit(solution)/shard_map/ppermute | solution.py:42
  80.5 9.2 %collective-permute-start.21 = (bf16[4,40,1280]{2,1,0:T(8,128)(2,1)S(1)}, bf16[4,40,1280]{2,1,0:T(8,128)(2,1)S(1)}, u32[]{:S(2)}, u32[]{:S(2)}) collective-permute-start(bf16[4,40,1280]{2,1,0:T(8,128)(2,1)S(1)} %get-tuple-element.31.refs_0_), channel_id=1, source_target_pairs={{0,32},{1,33},{2,34},{3,35},{4,36},{5,37},{6,38},{7,39},{8,40},{9,... | collective-permute-start | bytes 1228808 | tf_op jit(solution)/shard_map/ppermute | solution.py:42

commit v3 on v2

--- a/solution.py
+++ b/solution.py
@@ -11,8 +11,8 @@
 OUTER_RATE = 0.7
 DECAY = 0.9
 SCALE = OUTER_RATE * (1 + DECAY)
-AXES = ("zhi", "y", "x", "inner")
-SIZES = (2, 4, 4, 8)
+AXES = ("zhi", "y", "x", "zlo", "core")
+SIZES = (2, 4, 4, 4, 2)
 D = 2560
 HALF = D // 2
 ROWS = 20
@@ -134,6 +134,10 @@
         average = (own + other) * (1.0 / N_REP)
         momentum_out[:, cols] = DECAY * momentum[:, cols] + average
         master_out[:, cols] = base[:, cols] - SCALE * average
+
+
+def marked(out):
+    out[...] = jnp.zeros_like(out)
 
 
 def join(*refs):
@@ -203,10 +207,9 @@
     (new_b,) = call(
         functools.partial(new_rows, 0), outs, own_b, other_b, base, base_other, after=[new_a],
     )
-    all_a, all_b = call(
-        join, [like(FOUR, BF16)] * 2,
-        *received([new_a] * 4, "x", GATHER), *received([new_b] * 4, "y", GATHER),
-    )
+    a, b = received([new_a] * 4, "x", GATHER), received([new_b] * 4, "y", GATHER)
+    (mark,) = call(marked, [like((8, 128), F32)], after=a[1:])
+    all_a, all_b = call(join, [like(FOUR, BF16)] * 2, *a, *b, after=[swapped(mark, "core", 1)])
     master_out, momentum_out = call(
         new_state, [like((ROWS, D), F32)] * 2, own_a, other_a, own_b, other_b, base, momentum, after=[all_b],
     )
@@ -230,12 +233,12 @@
 
 def solution(mesh):
     parts = Mesh(mesh.devices.reshape(SIZES), AXES)
-    rep = ("zhi", "y", "x")
-    rows = P(("inner",) + rep, None)
+    rep, inner = ("zhi", "y", "x"), ("zlo", "core")
+    rows = P(inner + rep, None)
     return jax.shard_map(
         local,
         mesh=parts,
-        in_specs=(P(rep, "inner", None), rows, rows),
-        out_specs=(P("inner", None), rows, rows),
+        in_specs=(P(rep, inner, None), rows, rows),
+        out_specs=(P(inner, None), rows, rows),
         check_vma=False,
     )

time: 90.8 us -> 90.4 us (level)
  starting transfers between devices: 52.9 us -> 50.3 us
  waiting for transfers between devices: 29.4 us -> 30.9 us
    ppermute x27 -> x28, starting transfers between devices: 52.9 us -> 50.3 us  [moved(): return lax.ppermute(array, AXES, pairs)]
    ppermute x27 -> x28, waiting for transfers between devices: 29.4 us -> 30.9 us  [moved(): return lax.ppermute(array, AXES, pairs)]
    pallas_call x13 -> x14, Pallas kernels: 5.68 us -> 5.69 us  [call(): pl.pallas_call(kernel, out_shape=outs, in_specs=in_specs + [ANY] * len(af...]
  transfers between devices with their start and end apart: 27 -> 28, of which waited for: 14 -> 14; matrix products, arithmetic and copies ran while one was open for 0% -> 0% of each run, Pallas kernels for 5% -> 5%
where the time goes in v3:
time: 90.4 us; the launch traced here: 89.6 us
  starting transfers between devices  50.3 us (56%)
  waiting for transfers between devices  30.9 us (34%)
  Pallas kernels  5.69 us (6%)
  local copies, waits for them, and re-layouts  1.76 us (2%)
  between operations  0.97 us (1%)
    ppermute x28, starting transfers between devices, moved(): return lax.ppermute(array, AXES, pairs)  50.3 us
    ppermute x28, waiting for transfers between devices, moved(): return lax.ppermute(array, AXES, pairs)  30.9 us
    pallas_call x14, Pallas kernels, call(): pl.pallas_call(kernel, out_shape=outs, in_specs=in_specs + [ANY] * len(af...  5.69 us
  transfers between devices with their start and end apart: 28, of which 14 were waited for; matrix products, arithmetic and copies ran while one was open for 0% of the time, Pallas kernels for 5%

profile of v3, /device:TPU:32, one launch (start us, length us, event | category | flops | bytes accessed | tf_op | source)
XLA Modules:
  0.0 89.6 jit_solution(7328784083050168728)
XLA Ops:
  0.7 1.6 %dynamic-slice_bitcast_fusion = (bf16[80,2560]{1,0:T(8,128)(2,1)S(1)}, bf16[80,2560]{1,0:T(8,128)(2,1)S(1)}, bf16[80,2560]{1,0:T(8,128)(2,1)S(1)}, bf16[80,2560]{1,0:T(8,128)(2,1)S(1)}) fusion(bf16[8,80,2560]{2,1,0:T(8,128)(2,1)} %bitcast.13, s32[]{:T(128)S(6)} %select_n.39, s32[]{:T(128)S(6)} %select_n.37, s32[]{:T(128)S(6)} %select_n.35, s32[]{:T(128)S(6)} %select_n.33), kind=kLoop, calls=%fused_computation | loop fusion | bytes 3276816 | tf_op jit(solution)/shard_map/jit(dynamic_index_in_dim)/squeeze | solution.py:188
  2.3 1.7 %collective-permute-start = (bf16[80,2560]{1,0:T(8,128)(2,1)S(1)}, bf16[80,2560]{1,0:T(8,128)(2,1)S(1)}, u32[]{:S(2)}, u32[]{:S(2)}) collective-permute-start(bf16[80,2560]{1,0:T(8,128)(2,1)S(1)} %get-tuple-element.37), channel_id=1, source_target_pairs={{0,32},{1,33},{2,34},{3,35},{4,36},{5,37},{6,38},{7,39},{8,40},{9,... | collective-permute-start | bytes 1228808 | tf_op jit(solution)/shard_map/ppermute | solution.py:42
  4.0 1.7 %collective-permute-start.1 = (bf16[80,2560]{1,0:T(8,128)(2,1)S(1)}, bf16[80,2560]{1,0:T(8,128)(2,1)S(1)}, u32[]{:S(2)}, u32[]{:S(2)}) collective-permute-start(bf16[80,2560]{1,0:T(8,128)(2,1)S(1)} %get-tuple-element.36), channel_id=1, source_target_pairs={{0,96},{1,97},{2,98},{3,99},{4,100},{5,101},{6,102},{7,103},{8,104... | collective-permute-start | bytes 1228808 | tf_op jit(solution)/shard_map/ppermute | solution.py:42
  5.7 2.0 %collective-permute-start.2 = (bf16[80,2560]{1,0:T(8,128)(2,1)S(1)}, bf16[80,2560]{1,0:T(8,128)(2,1)S(1)}, u32[]{:S(2)}, u32[]{:S(2)}) collective-permute-start(bf16[80,2560]{1,0:T(8,128)(2,1)S(1)} %get-tuple-element.35), channel_id=1, source_target_pairs={{0,64},{1,65},{2,66},{3,67},{4,68},{5,69},{6,70},{7,71},{8,72},{9,... | collective-permute-start | bytes 1228808 | tf_op jit(solution)/shard_map/ppermute | solution.py:42
  8.0 1.6 %collective-permute-start.6 = (bf16[80,2560]{1,0:T(8,128)(2,1)S(1)}, bf16[80,2560]{1,0:T(8,128)(2,1)S(1)}, u32[]{:S(2)}, u32[]{:S(2)}) collective-permute-start(bf16[80,2560]{1,0:T(8,128)(2,1)S(1)} %get-tuple-element.24), channel_id=1, source_target_pairs={{0,8},{1,9},{2,10},{3,11},{4,12},{5,13},{6,14},{7,15},{8,16},{9,17... | collective-permute-start | bytes 1228808 | tf_op jit(solution)/shard_map/ppermute | solution.py:42
  9.6 1.7 %collective-permute-start.7 = (bf16[80,2560]{1,0:T(8,128)(2,1)S(1)}, bf16[80,2560]{1,0:T(8,128)(2,1)S(1)}, u32[]{:S(2)}, u32[]{:S(2)}) collective-permute-start(bf16[80,2560]{1,0:T(8,128)(2,1)S(1)} %get-tuple-element.25), channel_id=1, source_target_pairs={{0,24},{1,25},{2,26},{3,27},{4,28},{5,29},{6,30},{7,31},{8,0},{9,1... | collective-permute-start | bytes 1228808 | tf_op jit(solution)/shard_map/ppermute | solution.py:42
  11.3 3.6 %collective-permute-done.refs_1_.refs_2_ = bf16[80,2560]{1,0:T(8,128)(2,1)S(1)} collective-permute-done((bf16[80,2560]{1,0:T(8,128)(2,1)S(1)}, bf16[80,2560]{1,0:T(8,128)(2,1)S(1)}, u32[]{:S(2)}, u32[]{:S(2)}) %collective-permute-start) | collective-permute-done | bytes 409632 | tf_op jit(solution)/shard_map/ppermute | solution.py:42
  14.9 3.0 %collective-permute-start.8 = (bf16[80,2560]{1,0:T(8,128)(2,1)S(1)}, bf16[80,2560]{1,0:T(8,128)(2,1)S(1)}, u32[]{:S(2)}, u32[]{:S(2)}) collective-permute-start(bf16[80,2560]{1,0:T(8,128)(2,1)S(1)} %get-tuple-element.26), channel_id=1, source_target_pairs={{0,16},{1,17},{2,18},{3,19},{4,20},{5,21},{6,22},{7,23},{8,24},{9,... | collective-permute-start | bytes 1228808 | tf_op jit(solution)/shard_map/ppermute | solution.py:42
  18.0 5.1 %collective-permute-done.1.refs_2_ = bf16[80,2560]{1,0:T(8,128)(2,1)S(1)} collective-permute-done((bf16[80,2560]{1,0:T(8,128)(2,1)S(1)}, bf16[80,2560]{1,0:T(8,128)(2,1)S(1)}, u32[]{:S(2)}, u32[]{:S(2)}) %collective-permute-start.1) | collective-permute-done | bytes 409632 | tf_op jit(solution)/shard_map/ppermute | solution.py:42
  23.1 6.3 %collective-permute-start.9 = (f32[20,2560]{1,0:T(8,128)S(1)}, f32[20,2560]{1,0:T(8,128)S(1)}, u32[]{:S(2)}, u32[]{:S(2)}) collective-permute-start(f32[20,2560]{1,0:T(8,128)S(1)} %shard_map.61.refs_2_.refs_4_), channel_id=1, source_target_pairs={{0,128},{1,129},{2,130},{3,131},{4,132},{5,133},{6,134},{7,135},{8... | collective-permute-start | bytes 614408 | tf_op jit(solution)/shard_map/ppermute | solution.py:42
  29.8 1.6 %collective-permute-start.3 = (bf16[40,1280]{1,0:T(8,128)(2,1)S(1)}, bf16[40,1280]{1,0:T(8,128)(2,1)S(1)}, u32[]{:S(2)}, u32[]{:S(2)}) collective-permute-start(bf16[40,1280]{1,0:T(8,128)(2,1)S(1)} %get-tuple-element.20), channel_id=1, source_target_pairs={{0,8},{1,9},{2,10},{3,11},{4,12},{5,13},{6,14},{7,15},{8,16},{9,17... | collective-permute-start | bytes 307208 | tf_op jit(solution)/shard_map/ppermute | solution.py:42
  31.3 1.7 %collective-permute-start.4 = (bf16[40,1280]{1,0:T(8,128)(2,1)S(1)}, bf16[40,1280]{1,0:T(8,128)(2,1)S(1)}, u32[]{:S(2)}, u32[]{:S(2)}) collective-permute-start(bf16[40,1280]{1,0:T(8,128)(2,1)S(1)} %get-tuple-element.21), channel_id=1, source_target_pairs={{0,24},{1,25},{2,26},{3,27},{4,28},{5,29},{6,30},{7,31},{8,0},{9,1... | collective-permute-start | bytes 307208 | tf_op jit(solution)/shard_map/ppermute | solution.py:42
  33.1 1.8 %collective-permute-start.5 = (bf16[40,1280]{1,0:T(8,128)(2,1)S(1)}, bf16[40,1280]{1,0:T(8,128)(2,1)S(1)}, u32[]{:S(2)}, u32[]{:S(2)}) collective-permute-start(bf16[40,1280]{1,0:T(8,128)(2,1)S(1)} %get-tuple-element.22), channel_id=1, source_target_pairs={{0,16},{1,17},{2,18},{3,19},{4,20},{5,21},{6,22},{7,23},{8,24},{9,... | collective-permute-start | bytes 307208 | tf_op jit(solution)/shard_map/ppermute | solution.py:42
  35.7 3.7 %collective-permute-start.12 = (bf16[40,1280]{1,0:T(8,128)(2,1)S(1)}, bf16[40,1280]{1,0:T(8,128)(2,1)S(1)}, u32[]{:S(2)}, u32[]{:S(2)}) collective-permute-start(bf16[40,1280]{1,0:T(8,128)(2,1)S(1)} %get-tuple-element.29), channel_id=1, source_target_pairs={{0,96},{1,97},{2,98},{3,99},{4,100},{5,101},{6,102},{7,103},{8,104... | collective-permute-start | bytes 307208 | tf_op jit(solution)/shard_map/ppermute | solution.py:42
  39.4 2.7 %collective-permute-start.13 = (bf16[40,1280]{1,0:T(8,128)(2,1)S(1)}, bf16[40,1280]{1,0:T(8,128)(2,1)S(1)}, u32[]{:S(2)}, u32[]{:S(2)}) collective-permute-start(bf16[40,1280]{1,0:T(8,128)(2,1)S(1)} %get-tuple-element.30), channel_id=1, source_target_pairs={{0,64},{1,65},{2,66},{3,67},{4,68},{5,69},{6,70},{7,71},{8,72},{9,... | collective-permute-start | bytes 307208 | tf_op jit(solution)/shard_map/ppermute | solution.py:42
  42.2 3.3 %collective-permute-start.10 = (bf16[40,1280]{1,0:T(8,128)(2,1)S(1)}, bf16[40,1280]{1,0:T(8,128)(2,1)S(1)}, u32[]{:S(2)}, u32[]{:S(2)}) collective-permute-start(bf16[40,1280]{1,0:T(8,128)(2,1)S(1)} %shard_map.62.refs_4_.refs_0_), channel_id=1, source_target_pairs={{0,128},{1,129},{2,130},{3,131},{4,132},{5,133},{6,134},{7,135},{8... | collective-permute-start | bytes 307208 | tf_op jit(solution)/shard_map/ppermute | solution.py:42
  45.6 2.9 %collective-permute-start.17 = (bf16[40,1280]{1,0:T(8,128)(2,1)S(1)}, bf16[40,1280]{1,0:T(8,128)(2,1)S(1)}, u32[]{:S(2)}, u32[]{:S(2)}) collective-permute-start(bf16[40,1280]{1,0:T(8,128)(2,1)S(1)} %shard_map.63.refs_4_.refs_0_.refs_2_), channel_id=1, source_target_pairs={{0,128},{1,129},{2,130},{3,131},{4,132},{5,133},{6,134},{7,135},{8... | collective-permute-start | bytes 307208 | tf_op jit(solution)/shard_map/ppermute | solution.py:42
  48.5 3.5 %collective-permute-done.10.refs_1_ = bf16[40,1280]{1,0:T(8,128)(2,1)S(1)} collective-permute-done((bf16[40,1280]{1,0:T(8,128)(2,1)S(1)}, bf16[40,1280]{1,0:T(8,128)(2,1)S(1)}, u32[]{:S(2)}, u32[]{:S(2)}) %collective-permute-start.10) | collective-permute-done | bytes 102432 | tf_op jit(solution)/shard_map/ppermute | solution.py:42
  52.1 2.8 %collective-permute-start.14 = (bf16[40,1280]{1,0:T(8,128)(2,1)S(1)}, bf16[40,1280]{1,0:T(8,128)(2,1)S(1)}, u32[]{:S(2)}, u32[]{:S(2)}) collective-permute-start(bf16[40,1280]{1,0:T(8,128)(2,1)S(1)} %shard_map.64.refs_4_.refs_0_), channel_id=1, source_target_pairs={{0,16},{1,17},{2,18},{3,19},{4,20},{5,21},{6,22},{7,23},{8,24},{9,... | collective-permute-start | bytes 307208 | tf_op jit(solution)/shard_map/ppermute | solution.py:42
  55.3 1.6 %collective-permute-start.16 = (bf16[40,1280]{1,0:T(8,128)(2,1)S(1)}, bf16[40,1280]{1,0:T(8,128)(2,1)S(1)}, u32[]{:S(2)}, u32[]{:S(2)}) collective-permute-start(bf16[40,1280]{1,0:T(8,128)(2,1)S(1)} %shard_map.64.refs_4_.refs_0_), channel_id=1, source_target_pairs={{0,8},{1,9},{2,10},{3,11},{4,12},{5,13},{6,14},{7,15},{8,16},{9,17... | collective-permute-start | bytes 307208 | tf_op jit(solution)/shard_map/ppermute | solution.py:42
  57.4 2.1 %collective-permute-start.19 = (bf16[40,1280]{1,0:T(8,128)(2,1)S(1)}, bf16[40,1280]{1,0:T(8,128)(2,1)S(1)}, u32[]{:S(2)}, u32[]{:S(2)}) collective-permute-start(bf16[40,1280]{1,0:T(8,128)(2,1)S(1)} %shard_map.65.refs_4_), channel_id=1, source_target_pairs={{0,96},{1,97},{2,98},{3,99},{4,100},{5,101},{6,102},{7,103},{8,104... | collective-permute-start | bytes 307208 | tf_op jit(solution)/shard_map/ppermute | solution.py:42
  59.9 1.3 %collective-permute-done.16.refs_2_.refs_3_ = bf16[40,1280]{1,0:T(8,128)(2,1)S(1)} collective-permute-done((bf16[40,1280]{1,0:T(8,128)(2,1)S(1)}, bf16[40,1280]{1,0:T(8,128)(2,1)S(1)}, u32[]{:S(2)}, u32[]{:S(2)}) %collective-permute-start.16) | collective-permute-done | bytes 102432 | tf_op jit(solution)/shard_map/ppermute | solution.py:42
  61.2 2.1 %collective-permute-done.18.refs_5_ = bf16[40,1280]{1,0:T(8,128)(2,1)S(1)} collective-permute-done((bf16[40,1280]{1,0:T(8,128)(2,1)S(1)}, bf16[40,1280]{1,0:T(8,128)(2,1)S(1)}, u32[]{:S(2)}, u32[]{:S(2)}) %collective-permute-start.18) | collective-permute-done | bytes 102432 | tf_op jit(solution)/shard_map/ppermute | solution.py:42
  63.3 2.0 %collective-permute-done.20.refs_7_ = bf16[40,1280]{1,0:T(8,128)(2,1)S(1)} collective-permute-done((bf16[40,1280]{1,0:T(8,128)(2,1)S(1)}, bf16[40,1280]{1,0:T(8,128)(2,1)S(1)}, u32[]{:S(2)}, u32[]{:S(2)}) %collective-permute-start.20) | collective-permute-done | bytes 102432 | tf_op jit(solution)/shard_map/ppermute | solution.py:42
  65.4 2.6 %collective-permute-start.25 = (bf16[4,40,1280]{2,1,0:T(8,128)(2,1)S(1)}, bf16[4,40,1280]{2,1,0:T(8,128)(2,1)S(1)}, u32[]{:S(2)}, u32[]{:S(2)}) collective-permute-start(bf16[4,40,1280]{2,1,0:T(8,128)(2,1)S(1)} %get-tuple-element.32.refs_0_.refs_6_), channel_id=1, source_target_pairs={{0,16},{1,17},{2,18},{3,19},{4,20},{5,21},{6,22},{7,23},{8,24},{9,... | collective-permute-start | bytes 1228808 | tf_op jit(solution)/shard_map/ppermute | solution.py:42
  68.4 1.5 %collective-permute-start.27 = (bf16[4,40,1280]{2,1,0:T(8,128)(2,1)S(1)}, bf16[4,40,1280]{2,1,0:T(8,128)(2,1)S(1)}, u32[]{:S(2)}, u32[]{:S(2)}) collective-permute-start(bf16[4,40,1280]{2,1,0:T(8,128)(2,1)S(1)} %get-tuple-element.32.refs_0_.refs_6_), channel_id=1, source_target_pairs={{0,8},{1,9},{2,10},{3,11},{4,12},{5,13},{6,14},{7,15},{8,16},{9,17... | collective-permute-start | bytes 1228808 | tf_op jit(solution)/shard_map/ppermute | solution.py:42
  70.6 2.1 %collective-permute-start.24 = (bf16[4,40,1280]{2,1,0:T(8,128)(2,1)S(1)}, bf16[4,40,1280]{2,1,0:T(8,128)(2,1)S(1)}, u32[]{:S(2)}, u32[]{:S(2)}) collective-permute-start(bf16[4,40,1280]{2,1,0:T(8,128)(2,1)S(1)} %get-tuple-element.31.refs_0_), channel_id=1, source_target_pairs={{0,96},{1,97},{2,98},{3,99},{4,100},{5,101},{6,102},{7,103},{8,104... | collective-permute-start | bytes 1228808 | tf_op jit(solution)/shard_map/ppermute | solution.py:42
  72.7 6.7 %collective-permute-done.25.refs_1_ = bf16[4,40,1280]{2,1,0:T(8,128)(2,1)S(1)} collective-permute-done((bf16[4,40,1280]{2,1,0:T(8,128)(2,1)S(1)}, bf16[4,40,1280]{2,1,0:T(8,128)(2,1)S(1)}, u32[]{:S(2)}, u32[]{:S(2)}) %collective-permute-start.25) | collective-permute-done | bytes 409632 | tf_op jit(solution)/shard_map/ppermute | solution.py:42
  80.3 3.9 %collective-permute-done.26.refs_2_ = bf16[4,40,1280]{2,1,0:T(8,128)(2,1)S(1)} collective-permute-done((bf16[4,40,1280]{2,1,0:T(8,128)(2,1)S(1)}, bf16[4,40,1280]{2,1,0:T(8,128)(2,1)S(1)}, u32[]{:S(2)}, u32[]{:S(2)}) %collective-permute-start.26) | collective-permute-done | bytes 409632 | tf_op jit(solution)/shard_map/ppermute | solution.py:42
  84.3 1.3 %shard_map.68.refs_3_ = bf16[8,80,2560]{2,1,0:T(8,128)(2,1)} custom-call(bf16[4,40,1280]{2,1,0:T(8,128)(2,1)S(1)} %get-tuple-element.32.refs_0_.refs_6_, bf16[4,40,1280]{2,1,0:T(8,128)(2,1)S(1)} %collective-permute-done.25.refs_1_, bf16[4,40,1280]{2,1,0:T(8,128)(2,1)S(1)} %collective-permute-done.26.refs_2_, ...), custom_call_target="tpu_custom_call" | custom-call | flops 4915200 | bytes 4915200 | tf_op jit(solution)/shard_map/pallas_call | solution.py:66
  85.7 1.2 %collective-permute-done.24.refs_2_ = bf16[4,40,1280]{2,1,0:T(8,128)(2,1)S(1)} collective-permute-done((bf16[4,40,1280]{2,1,0:T(8,128)(2,1)S(1)}, bf16[4,40,1280]{2,1,0:T(8,128)(2,1)S(1)}, u32[]{:S(2)}, u32[]{:S(2)}) %collective-permute-start.24) | collective-permute-done | bytes 409632 | tf_op jit(solution)/shard_map/ppermute | solution.py:42
  86.9 1.2 %shard_map.69.refs_1_ = bf16[8,80,2560]{2,1,0:T(8,128)(2,1)} custom-call(bf16[4,40,1280]{2,1,0:T(8,128)(2,1)S(1)} %get-tuple-element.31.refs_0_, bf16[4,40,1280]{2,1,0:T(8,128)(2,1)S(1)} %collective-permute-done.23.refs_1_, bf16[4,40,1280]{2,1,0:T(8,128)(2,1)S(1)} %collective-permute-done.24.refs_2_, ...), custom_call_target="tpu_custom_call", output_to_operand_aliasing={{}: (3, {})} | custom-call | flops 7782400 | bytes 7782400 | tf_op jit(solution)/shard_map/pallas_call | solution.py:66
  (46 shorter events, 6.8 us)
Async XLA Ops:
  0.6 7.0 %copy-start.2 = (bf16[1,640,2560]{2,1,0:T(8,128)(2,1)S(1)}, bf16[1,640,2560]{2,1,0:T(8,128)(2,1)}, u32[]{:S(2)}) copy-start(bf16[1,640,2560]{2,1,0:T(8,128)(2,1)} %param.3) | copy-start | bytes 9830404
  2.3 15.6 %copy-start = (f32[20,2560]{1,0:T(8,128)S(1)}, f32[20,2560]{1,0:T(8,128)}, u32[]{:S(2)}) copy-start(f32[20,2560]{1,0:T(8,128)} %refs_5_.1) | copy-start | bytes 614404
  2.3 15.6 %copy-start.1 = (f32[20,2560]{1,0:T(8,128)S(1)}, f32[20,2560]{1,0:T(8,128)}, u32[]{:S(2)}) copy-start(f32[20,2560]{1,0:T(8,128)} %refs_0_.1) | copy-start | bytes 614404
  2.3 12.6 %collective-permute-start = (bf16[80,2560]{1,0:T(8,128)(2,1)S(1)}, bf16[80,2560]{1,0:T(8,128)(2,1)S(1)}, u32[]{:S(2)}, u32[]{:S(2)}) collective-permute-start(bf16[80,2560]{1,0:T(8,128)(2,1)S(1)} %get-tuple-element.37), channel_id=1, source_target_pairs={{0,32},{1,33},{2,34},{3,35},{4,36},{5,37},{6,38},{7,39},{8,40},{9,... | collective-permute-start | bytes 1228808 | tf_op jit(solution)/shard_map/ppermute | solution.py:42
  4.0 19.1 %collective-permute-start.1 = (bf16[80,2560]{1,0:T(8,128)(2,1)S(1)}, bf16[80,2560]{1,0:T(8,128)(2,1)S(1)}, u32[]{:S(2)}, u32[]{:S(2)}) collective-permute-start(bf16[80,2560]{1,0:T(8,128)(2,1)S(1)} %get-tuple-element.36), channel_id=1, source_target_pairs={{0,96},{1,97},{2,98},{3,99},{4,100},{5,101},{6,102},{7,103},{8,104... | collective-permute-start | bytes 1228808 | tf_op jit(solution)/shard_map/ppermute | solution.py:42
  5.7 23.7 %collective-permute-start.2 = (bf16[80,2560]{1,0:T(8,128)(2,1)S(1)}, bf16[80,2560]{1,0:T(8,128)(2,1)S(1)}, u32[]{:S(2)}, u32[]{:S(2)}) collective-permute-start(bf16[80,2560]{1,0:T(8,128)(2,1)S(1)} %get-tuple-element.35), channel_id=1, source_target_pairs={{0,64},{1,65},{2,66},{3,67},{4,68},{5,69},{6,70},{7,71},{8,72},{9,... | collective-permute-start | bytes 1228808 | tf_op jit(solution)/shard_map/ppermute | solution.py:42
  8.0 23.3 %collective-permute-start.6 = (bf16[80,2560]{1,0:T(8,128)(2,1)S(1)}, bf16[80,2560]{1,0:T(8,128)(2,1)S(1)}, u32[]{:S(2)}, u32[]{:S(2)}) collective-permute-start(bf16[80,2560]{1,0:T(8,128)(2,1)S(1)} %get-tuple-element.24), channel_id=1, source_target_pairs={{0,8},{1,9},{2,10},{3,11},{4,12},{5,13},{6,14},{7,15},{8,16},{9,17... | collective-permute-start | bytes 1228808 | tf_op jit(solution)/shard_map/ppermute | solution.py:42
  9.6 23.5 %collective-permute-start.7 = (bf16[80,2560]{1,0:T(8,128)(2,1)S(1)}, bf16[80,2560]{1,0:T(8,128)(2,1)S(1)}, u32[]{:S(2)}, u32[]{:S(2)}) collective-permute-start(bf16[80,2560]{1,0:T(8,128)(2,1)S(1)} %get-tuple-element.25), channel_id=1, source_target_pairs={{0,24},{1,25},{2,26},{3,27},{4,28},{5,29},{6,30},{7,31},{8,0},{9,1... | collective-permute-start | bytes 1228808 | tf_op jit(solution)/shard_map/ppermute | solution.py:42
  14.9 20.0 %collective-permute-start.8 = (bf16[80,2560]{1,0:T(8,128)(2,1)S(1)}, bf16[80,2560]{1,0:T(8,128)(2,1)S(1)}, u32[]{:S(2)}, u32[]{:S(2)}) collective-permute-start(bf16[80,2560]{1,0:T(8,128)(2,1)S(1)} %get-tuple-element.26), channel_id=1, source_target_pairs={{0,16},{1,17},{2,18},{3,19},{4,20},{5,21},{6,22},{7,23},{8,24},{9,... | collective-permute-start | bytes 1228808 | tf_op jit(solution)/shard_map/ppermute | solution.py:42
  23.1 19.1 %collective-permute-start.9 = (f32[20,2560]{1,0:T(8,128)S(1)}, f32[20,2560]{1,0:T(8,128)S(1)}, u32[]{:S(2)}, u32[]{:S(2)}) collective-permute-start(f32[20,2560]{1,0:T(8,128)S(1)} %shard_map.61.refs_2_.refs_4_), channel_id=1, source_target_pairs={{0,128},{1,129},{2,130},{3,131},{4,132},{5,133},{6,134},{7,135},{8... | collective-permute-start | bytes 614408 | tf_op jit(solution)/shard_map/ppermute | solution.py:42
  29.8 5.9 %collective-permute-start.3 = (bf16[40,1280]{1,0:T(8,128)(2,1)S(1)}, bf16[40,1280]{1,0:T(8,128)(2,1)S(1)}, u32[]{:S(2)}, u32[]{:S(2)}) collective-permute-start(bf16[40,1280]{1,0:T(8,128)(2,1)S(1)} %get-tuple-element.20), channel_id=1, source_target_pairs={{0,8},{1,9},{2,10},{3,11},{4,12},{5,13},{6,14},{7,15},{8,16},{9,17... | collective-permute-start | bytes 307208 | tf_op jit(solution)/shard_map/ppermute | solution.py:42
  31.3 8.0 %collective-permute-start.4 = (bf16[40,1280]{1,0:T(8,128)(2,1)S(1)}, bf16[40,1280]{1,0:T(8,128)(2,1)S(1)}, u32[]{:S(2)}, u32[]{:S(2)}) collective-permute-start(bf16[40,1280]{1,0:T(8,128)(2,1)S(1)} %get-tuple-element.21), channel_id=1, source_target_pairs={{0,24},{1,25},{2,26},{3,27},{4,28},{5,29},{6,30},{7,31},{8,0},{9,1... | collective-permute-start | bytes 307208 | tf_op jit(solution)/shard_map/ppermute | solution.py:42
  33.1 9.0 %collective-permute-start.5 = (bf16[40,1280]{1,0:T(8,128)(2,1)S(1)}, bf16[40,1280]{1,0:T(8,128)(2,1)S(1)}, u32[]{:S(2)}, u32[]{:S(2)}) collective-permute-start(bf16[40,1280]{1,0:T(8,128)(2,1)S(1)} %get-tuple-element.22), channel_id=1, source_target_pairs={{0,16},{1,17},{2,18},{3,19},{4,20},{5,21},{6,22},{7,23},{8,24},{9,... | collective-permute-start | bytes 307208 | tf_op jit(solution)/shard_map/ppermute | solution.py:42
  35.3 10.1 %collective-permute-start.11 = (bf16[40,1280]{1,0:T(8,128)(2,1)S(1)}, bf16[40,1280]{1,0:T(8,128)(2,1)S(1)}, u32[]{:S(2)}, u32[]{:S(2)}) collective-permute-start(bf16[40,1280]{1,0:T(8,128)(2,1)S(1)} %get-tuple-element.28), channel_id=1, source_target_pairs={{0,32},{1,33},{2,34},{3,35},{4,36},{5,37},{6,38},{7,39},{8,40},{9,... | collective-permute-start | bytes 307208 | tf_op jit(solution)/shard_map/ppermute | solution.py:42
  35.7 9.7 %collective-permute-start.12 = (bf16[40,1280]{1,0:T(8,128)(2,1)S(1)}, bf16[40,1280]{1,0:T(8,128)(2,1)S(1)}, u32[]{:S(2)}, u32[]{:S(2)}) collective-permute-start(bf16[40,1280]{1,0:T(8,128)(2,1)S(1)} %get-tuple-element.29), channel_id=1, source_target_pairs={{0,96},{1,97},{2,98},{3,99},{4,100},{5,101},{6,102},{7,103},{8,104... | collective-permute-start | bytes 307208 | tf_op jit(solution)/shard_map/ppermute | solution.py:42
  39.4 6.2 %collective-permute-start.13 = (bf16[40,1280]{1,0:T(8,128)(2,1)S(1)}, bf16[40,1280]{1,0:T(8,128)(2,1)S(1)}, u32[]{:S(2)}, u32[]{:S(2)}) collective-permute-start(bf16[40,1280]{1,0:T(8,128)(2,1)S(1)} %get-tuple-element.30), channel_id=1, source_target_pairs={{0,64},{1,65},{2,66},{3,67},{4,68},{5,69},{6,70},{7,71},{8,72},{9,... | collective-permute-start | bytes 307208 | tf_op jit(solution)/shard_map/ppermute | solution.py:42
  42.2 9.9 %collective-permute-start.10 = (bf16[40,1280]{1,0:T(8,128)(2,1)S(1)}, bf16[40,1280]{1,0:T(8,128)(2,1)S(1)}, u32[]{:S(2)}, u32[]{:S(2)}) collective-permute-start(bf16[40,1280]{1,0:T(8,128)(2,1)S(1)} %shard_map.62.refs_4_.refs_0_), channel_id=1, source_target_pairs={{0,128},{1,129},{2,130},{3,131},{4,132},{5,133},{6,134},{7,135},{8... | collective-permute-start | bytes 307208 | tf_op jit(solution)/shard_map/ppermute | solution.py:42
  45.6 11.4 %collective-permute-start.17 = (bf16[40,1280]{1,0:T(8,128)(2,1)S(1)}, bf16[40,1280]{1,0:T(8,128)(2,1)S(1)}, u32[]{:S(2)}, u32[]{:S(2)}) collective-permute-start(bf16[40,1280]{1,0:T(8,128)(2,1)S(1)} %shard_map.63.refs_4_.refs_0_.refs_2_), channel_id=1, source_target_pairs={{0,128},{1,129},{2,130},{3,131},{4,132},{5,133},{6,134},{7,135},{8... | collective-permute-start | bytes 307208 | tf_op jit(solution)/shard_map/ppermute | solution.py:42
  52.1 7.3 %collective-permute-start.14 = (bf16[40,1280]{1,0:T(8,128)(2,1)S(1)}, bf16[40,1280]{1,0:T(8,128)(2,1)S(1)}, u32[]{:S(2)}, u32[]{:S(2)}) collective-permute-start(bf16[40,1280]{1,0:T(8,128)(2,1)S(1)} %shard_map.64.refs_4_.refs_0_), channel_id=1, source_target_pairs={{0,16},{1,17},{2,18},{3,19},{4,20},{5,21},{6,22},{7,23},{8,24},{9,... | collective-permute-start | bytes 307208 | tf_op jit(solution)/shard_map/ppermute | solution.py:42
  55.0 4.9 %collective-permute-start.15 = (bf16[40,1280]{1,0:T(8,128)(2,1)S(1)}, bf16[40,1280]{1,0:T(8,128)(2,1)S(1)}, u32[]{:S(2)}, u32[]{:S(2)}) collective-permute-start(bf16[40,1280]{1,0:T(8,128)(2,1)S(1)} %shard_map.64.refs_4_.refs_0_), channel_id=1, source_target_pairs={{0,24},{1,25},{2,26},{3,27},{4,28},{5,29},{6,30},{7,31},{8,0},{9,1... | collective-permute-start | bytes 307208 | tf_op jit(solution)/shard_map/ppermute | solution.py:42
  55.3 5.9 %collective-permute-start.16 = (bf16[40,1280]{1,0:T(8,128)(2,1)S(1)}, bf16[40,1280]{1,0:T(8,128)(2,1)S(1)}, u32[]{:S(2)}, u32[]{:S(2)}) collective-permute-start(bf16[40,1280]{1,0:T(8,128)(2,1)S(1)} %shard_map.64.refs_4_.refs_0_), channel_id=1, source_target_pairs={{0,8},{1,9},{2,10},{3,11},{4,12},{5,13},{6,14},{7,15},{8,16},{9,17... | collective-permute-start | bytes 307208 | tf_op jit(solution)/shard_map/ppermute | solution.py:42
  57.1 6.3 %collective-permute-start.18 = (bf16[40,1280]{1,0:T(8,128)(2,1)S(1)}, bf16[40,1280]{1,0:T(8,128)(2,1)S(1)}, u32[]{:S(2)}, u32[]{:S(2)}) collective-permute-start(bf16[40,1280]{1,0:T(8,128)(2,1)S(1)} %shard_map.65.refs_4_), channel_id=1, source_target_pairs={{0,64},{1,65},{2,66},{3,67},{4,68},{5,69},{6,70},{7,71},{8,72},{9,... | collective-permute-start | bytes 307208 | tf_op jit(solution)/shard_map/ppermute | solution.py:42
  57.4 6.0 %collective-permute-start.19 = (bf16[40,1280]{1,0:T(8,128)(2,1)S(1)}, bf16[40,1280]{1,0:T(8,128)(2,1)S(1)}, u32[]{:S(2)}, u32[]{:S(2)}) collective-permute-start(bf16[40,1280]{1,0:T(8,128)(2,1)S(1)} %shard_map.65.refs_4_), channel_id=1, source_target_pairs={{0,96},{1,97},{2,98},{3,99},{4,100},{5,101},{6,102},{7,103},{8,104... | collective-permute-start | bytes 307208 | tf_op jit(solution)/shard_map/ppermute | solution.py:42
  59.4 5.9 %collective-permute-start.20 = (bf16[40,1280]{1,0:T(8,128)(2,1)S(1)}, bf16[40,1280]{1,0:T(8,128)(2,1)S(1)}, u32[]{:S(2)}, u32[]{:S(2)}) collective-permute-start(bf16[40,1280]{1,0:T(8,128)(2,1)S(1)} %shard_map.65.refs_4_), channel_id=1, source_target_pairs={{0,32},{1,33},{2,34},{3,35},{4,36},{5,37},{6,38},{7,39},{8,40},{9,... | collective-permute-start | bytes 307208 | tf_op jit(solution)/shard_map/ppermute | solution.py:42
  61.2 4.1 %collective-permute-start.21 = (f32[8,128]{1,0:T(8,128)S(1)}, f32[8,128]{1,0:T(8,128)S(1)}, u32[]{:S(2)}, u32[]{:S(2)}) collective-permute-start(f32[8,128]{1,0:T(8,128)S(1)} %shard_map.66), channel_id=1, source_target_pairs={{0,1},{1,0},{2,3},{3,2},{4,5},{5,4},{6,7},{7,6},{8,9},{9,8},{10,11... | collective-permute-start | bytes 12296 | tf_op jit(solution)/shard_map/ppermute | solution.py:42
  65.4 14.0 %collective-permute-start.25 = (bf16[4,40,1280]{2,1,0:T(8,128)(2,1)S(1)}, bf16[4,40,1280]{2,1,0:T(8,128)(2,1)S(1)}, u32[]{:S(2)}, u32[]{:S(2)}) collective-permute-start(bf16[4,40,1280]{2,1,0:T(8,128)(2,1)S(1)} %get-tuple-element.32.refs_0_.refs_6_), channel_id=1, source_target_pairs={{0,16},{1,17},{2,18},{3,19},{4,20},{5,21},{6,22},{7,23},{8,24},{9,... | collective-permute-start | bytes 1228808 | tf_op jit(solution)/shard_map/ppermute | solution.py:42
  67.9 16.3 %collective-permute-start.26 = (bf16[4,40,1280]{2,1,0:T(8,128)(2,1)S(1)}, bf16[4,40,1280]{2,1,0:T(8,128)(2,1)S(1)}, u32[]{:S(2)}, u32[]{:S(2)}) collective-permute-start(bf16[4,40,1280]{2,1,0:T(8,128)(2,1)S(1)} %get-tuple-element.32.refs_0_.refs_6_), channel_id=1, source_target_pairs={{0,24},{1,25},{2,26},{3,27},{4,28},{5,29},{6,30},{7,31},{8,0},{9,1... | collective-permute-start | bytes 1228808 | tf_op jit(solution)/shard_map/ppermute | solution.py:42
  68.4 15.9 %collective-permute-start.27 = (bf16[4,40,1280]{2,1,0:T(8,128)(2,1)S(1)}, bf16[4,40,1280]{2,1,0:T(8,128)(2,1)S(1)}, u32[]{:S(2)}, u32[]{:S(2)}) collective-permute-start(bf16[4,40,1280]{2,1,0:T(8,128)(2,1)S(1)} %get-tuple-element.32.refs_0_.refs_6_), channel_id=1, source_target_pairs={{0,8},{1,9},{2,10},{3,11},{4,12},{5,13},{6,14},{7,15},{8,16},{9,17... | collective-permute-start | bytes 1228808 | tf_op jit(solution)/shard_map/ppermute | solution.py:42
  69.9 15.7 %collective-permute-start.23 = (bf16[4,40,1280]{2,1,0:T(8,128)(2,1)S(1)}, bf16[4,40,1280]{2,1,0:T(8,128)(2,1)S(1)}, u32[]{:S(2)}, u32[]{:S(2)}) collective-permute-start(bf16[4,40,1280]{2,1,0:T(8,128)(2,1)S(1)} %get-tuple-element.31.refs_0_), channel_id=1, source_target_pairs={{0,64},{1,65},{2,66},{3,67},{4,68},{5,69},{6,70},{7,71},{8,72},{9,... | collective-permute-start | bytes 1228808 | tf_op jit(solution)/shard_map/ppermute | solution.py:42
  70.6 16.3 %collective-permute-start.24 = (bf16[4,40,1280]{2,1,0:T(8,128)(2,1)S(1)}, bf16[4,40,1280]{2,1,0:T(8,128)(2,1)S(1)}, u32[]{:S(2)}, u32[]{:S(2)}) collective-permute-start(bf16[4,40,1280]{2,1,0:T(8,128)(2,1)S(1)} %get-tuple-element.31.refs_0_), channel_id=1, source_target_pairs={{0,96},{1,97},{2,98},{3,99},{4,100},{5,101},{6,102},{7,103},{8,104... | collective-permute-start | bytes 1228808 | tf_op jit(solution)/shard_map/ppermute | solution.py:42
  79.4 9.2 %collective-permute-start.22 = (bf16[4,40,1280]{2,1,0:T(8,128)(2,1)S(1)}, bf16[4,40,1280]{2,1,0:T(8,128)(2,1)S(1)}, u32[]{:S(2)}, u32[]{:S(2)}) collective-permute-start(bf16[4,40,1280]{2,1,0:T(8,128)(2,1)S(1)} %get-tuple-element.31.refs_0_), channel_id=1, source_target_pairs={{0,32},{1,33},{2,34},{3,35},{4,36},{5,37},{6,38},{7,39},{8,40},{9,... | collective-permute-start | bytes 1228808 | tf_op jit(solution)/shard_map/ppermute | solution.py:42

commit v4 on v3

--- a/solution.py
+++ b/solution.py
@@ -188,7 +188,7 @@
     a = [lax.dynamic_index_in_dim(d, 4 + (y + s) % 4, keepdims=False) for s in range(4)]
     b = call(pack_rows, [big] * 4, d[:4])
     a = received(a, "y", FIRST)
-    b = received(b, "x", FIRST)
+    b = received(b, "x", LAST)
     (base,) = call(early_base, [like((ROWS, D), F32)], master, momentum, after=[a[1]])
     base_other = swapped(base, "zhi", 1)
 

time: 90.4 us -> 90.1 us (level)
  no operation moved by 1% of the time
where the time goes in v4:
time: 90.1 us; the launch traced here: 89.6 us
  starting transfers between devices  50.3 us (56%)
  waiting for transfers between devices  30.8 us (34%)
  Pallas kernels  5.69 us (6%)
  local copies, waits for them, and re-layouts  1.76 us (2%)
  between operations  0.97 us (1%)
    ppermute x28, starting transfers between devices, moved(): return lax.ppermute(array, AXES, pairs)  50.3 us
    ppermute x28, waiting for transfers between devices, moved(): return lax.ppermute(array, AXES, pairs)  30.8 us
    pallas_call x14, Pallas kernels, call(): pl.pallas_call(kernel, out_shape=outs, in_specs=in_specs + [ANY] * len(af...  5.69 us
  transfers between devices with their start and end apart: 28, of which 14 were waited for; matrix products, arithmetic and copies ran while one was open for 0% of the time, Pallas kernels for 5%

profile of v4, /device:TPU:32, one launch (start us, length us, event | category | flops | bytes accessed | tf_op | source)
XLA Modules:
  0.0 89.6 jit_solution(7039621883975247459)
XLA Ops:
  0.7 1.6 %dynamic-slice_bitcast_fusion = (bf16[80,2560]{1,0:T(8,128)(2,1)S(1)}, bf16[80,2560]{1,0:T(8,128)(2,1)S(1)}, bf16[80,2560]{1,0:T(8,128)(2,1)S(1)}, bf16[80,2560]{1,0:T(8,128)(2,1)S(1)}) fusion(bf16[8,80,2560]{2,1,0:T(8,128)(2,1)} %bitcast.13, s32[]{:T(128)S(6)} %select_n.39, s32[]{:T(128)S(6)} %select_n.37, s32[]{:T(128)S(6)} %select_n.35, s32[]{:T(128)S(6)} %select_n.33), kind=kLoop, calls=%fused_computation | loop fusion | bytes 3276816 | tf_op jit(solution)/shard_map/jit(dynamic_index_in_dim)/squeeze | solution.py:188
  2.3 1.7 %collective-permute-start = (bf16[80,2560]{1,0:T(8,128)(2,1)S(1)}, bf16[80,2560]{1,0:T(8,128)(2,1)S(1)}, u32[]{:S(2)}, u32[]{:S(2)}) collective-permute-start(bf16[80,2560]{1,0:T(8,128)(2,1)S(1)} %get-tuple-element.37), channel_id=1, source_target_pairs={{0,32},{1,33},{2,34},{3,35},{4,36},{5,37},{6,38},{7,39},{8,40},{9,... | collective-permute-start | bytes 1228808 | tf_op jit(solution)/shard_map/ppermute | solution.py:42
  4.0 1.7 %collective-permute-start.1 = (bf16[80,2560]{1,0:T(8,128)(2,1)S(1)}, bf16[80,2560]{1,0:T(8,128)(2,1)S(1)}, u32[]{:S(2)}, u32[]{:S(2)}) collective-permute-start(bf16[80,2560]{1,0:T(8,128)(2,1)S(1)} %get-tuple-element.36), channel_id=1, source_target_pairs={{0,96},{1,97},{2,98},{3,99},{4,100},{5,101},{6,102},{7,103},{8,104... | collective-permute-start | bytes 1228808 | tf_op jit(solution)/shard_map/ppermute | solution.py:42
  5.7 2.0 %collective-permute-start.2 = (bf16[80,2560]{1,0:T(8,128)(2,1)S(1)}, bf16[80,2560]{1,0:T(8,128)(2,1)S(1)}, u32[]{:S(2)}, u32[]{:S(2)}) collective-permute-start(bf16[80,2560]{1,0:T(8,128)(2,1)S(1)} %get-tuple-element.35), channel_id=1, source_target_pairs={{0,64},{1,65},{2,66},{3,67},{4,68},{5,69},{6,70},{7,71},{8,72},{9,... | collective-permute-start | bytes 1228808 | tf_op jit(solution)/shard_map/ppermute | solution.py:42
  8.0 3.1 %collective-permute-start.6 = (bf16[80,2560]{1,0:T(8,128)(2,1)S(1)}, bf16[80,2560]{1,0:T(8,128)(2,1)S(1)}, u32[]{:S(2)}, u32[]{:S(2)}) collective-permute-start(bf16[80,2560]{1,0:T(8,128)(2,1)S(1)} %get-tuple-element.24), channel_id=1, source_target_pairs={{0,16},{1,17},{2,18},{3,19},{4,20},{5,21},{6,22},{7,23},{8,24},{9,... | collective-permute-start | bytes 1228808 | tf_op jit(solution)/shard_map/ppermute | solution.py:42
  11.1 1.1 %collective-permute-start.7 = (bf16[80,2560]{1,0:T(8,128)(2,1)S(1)}, bf16[80,2560]{1,0:T(8,128)(2,1)S(1)}, u32[]{:S(2)}, u32[]{:S(2)}) collective-permute-start(bf16[80,2560]{1,0:T(8,128)(2,1)S(1)} %get-tuple-element.25), channel_id=1, source_target_pairs={{0,24},{1,25},{2,26},{3,27},{4,28},{5,29},{6,30},{7,31},{8,0},{9,1... | collective-permute-start | bytes 1228808 | tf_op jit(solution)/shard_map/ppermute | solution.py:42
  12.3 2.6 %collective-permute-done.refs_1_.refs_2_ = bf16[80,2560]{1,0:T(8,128)(2,1)S(1)} collective-permute-done((bf16[80,2560]{1,0:T(8,128)(2,1)S(1)}, bf16[80,2560]{1,0:T(8,128)(2,1)S(1)}, u32[]{:S(2)}, u32[]{:S(2)}) %collective-permute-start) | collective-permute-done | bytes 409632 | tf_op jit(solution)/shard_map/ppermute | solution.py:42
  14.9 1.5 %collective-permute-start.8 = (bf16[80,2560]{1,0:T(8,128)(2,1)S(1)}, bf16[80,2560]{1,0:T(8,128)(2,1)S(1)}, u32[]{:S(2)}, u32[]{:S(2)}) collective-permute-start(bf16[80,2560]{1,0:T(8,128)(2,1)S(1)} %get-tuple-element.26), channel_id=1, source_target_pairs={{0,8},{1,9},{2,10},{3,11},{4,12},{5,13},{6,14},{7,15},{8,16},{9,17... | collective-permute-start | bytes 1228808 | tf_op jit(solution)/shard_map/ppermute | solution.py:42
  16.4 6.6 %collective-permute-done.1.refs_2_ = bf16[80,2560]{1,0:T(8,128)(2,1)S(1)} collective-permute-done((bf16[80,2560]{1,0:T(8,128)(2,1)S(1)}, bf16[80,2560]{1,0:T(8,128)(2,1)S(1)}, u32[]{:S(2)}, u32[]{:S(2)}) %collective-permute-start.1) | collective-permute-done | bytes 409632 | tf_op jit(solution)/shard_map/ppermute | solution.py:42
  23.1 6.3 %collective-permute-start.9 = (f32[20,2560]{1,0:T(8,128)S(1)}, f32[20,2560]{1,0:T(8,128)S(1)}, u32[]{:S(2)}, u32[]{:S(2)}) collective-permute-start(f32[20,2560]{1,0:T(8,128)S(1)} %shard_map.61.refs_2_.refs_4_), channel_id=1, source_target_pairs={{0,128},{1,129},{2,130},{3,131},{4,132},{5,133},{6,134},{7,135},{8... | collective-permute-start | bytes 614408 | tf_op jit(solution)/shard_map/ppermute | solution.py:42
  29.8 1.6 %collective-permute-start.3 = (bf16[40,1280]{1,0:T(8,128)(2,1)S(1)}, bf16[40,1280]{1,0:T(8,128)(2,1)S(1)}, u32[]{:S(2)}, u32[]{:S(2)}) collective-permute-start(bf16[40,1280]{1,0:T(8,128)(2,1)S(1)} %get-tuple-element.20), channel_id=1, source_target_pairs={{0,8},{1,9},{2,10},{3,11},{4,12},{5,13},{6,14},{7,15},{8,16},{9,17... | collective-permute-start | bytes 307208 | tf_op jit(solution)/shard_map/ppermute | solution.py:42
  31.3 1.7 %collective-permute-start.4 = (bf16[40,1280]{1,0:T(8,128)(2,1)S(1)}, bf16[40,1280]{1,0:T(8,128)(2,1)S(1)}, u32[]{:S(2)}, u32[]{:S(2)}) collective-permute-start(bf16[40,1280]{1,0:T(8,128)(2,1)S(1)} %get-tuple-element.21), channel_id=1, source_target_pairs={{0,24},{1,25},{2,26},{3,27},{4,28},{5,29},{6,30},{7,31},{8,0},{9,1... | collective-permute-start | bytes 307208 | tf_op jit(solution)/shard_map/ppermute | solution.py:42
  33.1 1.8 %collective-permute-start.5 = (bf16[40,1280]{1,0:T(8,128)(2,1)S(1)}, bf16[40,1280]{1,0:T(8,128)(2,1)S(1)}, u32[]{:S(2)}, u32[]{:S(2)}) collective-permute-start(bf16[40,1280]{1,0:T(8,128)(2,1)S(1)} %get-tuple-element.22), channel_id=1, source_target_pairs={{0,16},{1,17},{2,18},{3,19},{4,20},{5,21},{6,22},{7,23},{8,24},{9,... | collective-permute-start | bytes 307208 | tf_op jit(solution)/shard_map/ppermute | solution.py:42
  35.7 3.7 %collective-permute-start.12 = (bf16[40,1280]{1,0:T(8,128)(2,1)S(1)}, bf16[40,1280]{1,0:T(8,128)(2,1)S(1)}, u32[]{:S(2)}, u32[]{:S(2)}) collective-permute-start(bf16[40,1280]{1,0:T(8,128)(2,1)S(1)} %get-tuple-element.29), channel_id=1, source_target_pairs={{0,96},{1,97},{2,98},{3,99},{4,100},{5,101},{6,102},{7,103},{8,104... | collective-permute-start | bytes 307208 | tf_op jit(solution)/shard_map/ppermute | solution.py:42
  39.4 1.9 %collective-permute-start.13 = (bf16[40,1280]{1,0:T(8,128)(2,1)S(1)}, bf16[40,1280]{1,0:T(8,128)(2,1)S(1)}, u32[]{:S(2)}, u32[]{:S(2)}) collective-permute-start(bf16[40,1280]{1,0:T(8,128)(2,1)S(1)} %get-tuple-element.30), channel_id=1, source_target_pairs={{0,64},{1,65},{2,66},{3,67},{4,68},{5,69},{6,70},{7,71},{8,72},{9,... | collective-permute-start | bytes 307208 | tf_op jit(solution)/shard_map/ppermute | solution.py:42
  41.4 3.4 %collective-permute-start.10 = (bf16[40,1280]{1,0:T(8,128)(2,1)S(1)}, bf16[40,1280]{1,0:T(8,128)(2,1)S(1)}, u32[]{:S(2)}, u32[]{:S(2)}) collective-permute-start(bf16[40,1280]{1,0:T(8,128)(2,1)S(1)} %shard_map.62.refs_4_.refs_0_), channel_id=1, source_target_pairs={{0,128},{1,129},{2,130},{3,131},{4,132},{5,133},{6,134},{7,135},{8... | collective-permute-start | bytes 307208 | tf_op jit(solution)/shard_map/ppermute | solution.py:42
  45.6 2.1 %collective-permute-start.17 = (bf16[40,1280]{1,0:T(8,128)(2,1)S(1)}, bf16[40,1280]{1,0:T(8,128)(2,1)S(1)}, u32[]{:S(2)}, u32[]{:S(2)}) collective-permute-start(bf16[40,1280]{1,0:T(8,128)(2,1)S(1)} %shard_map.63.refs_4_.refs_0_.refs_2_), channel_id=1, source_target_pairs={{0,128},{1,129},{2,130},{3,131},{4,132},{5,133},{6,134},{7,135},{8... | collective-permute-start | bytes 307208 | tf_op jit(solution)/shard_map/ppermute | solution.py:42
  47.7 3.1 %collective-permute-done.10.refs_1_ = bf16[40,1280]{1,0:T(8,128)(2,1)S(1)} collective-permute-done((bf16[40,1280]{1,0:T(8,128)(2,1)S(1)}, bf16[40,1280]{1,0:T(8,128)(2,1)S(1)}, u32[]{:S(2)}, u32[]{:S(2)}) %collective-permute-start.10) | collective-permute-done | bytes 102432 | tf_op jit(solution)/shard_map/ppermute | solution.py:42
  50.9 2.5 %collective-permute-start.14 = (bf16[40,1280]{1,0:T(8,128)(2,1)S(1)}, bf16[40,1280]{1,0:T(8,128)(2,1)S(1)}, u32[]{:S(2)}, u32[]{:S(2)}) collective-permute-start(bf16[40,1280]{1,0:T(8,128)(2,1)S(1)} %shard_map.64.refs_4_.refs_0_), channel_id=1, source_target_pairs={{0,16},{1,17},{2,18},{3,19},{4,20},{5,21},{6,22},{7,23},{8,24},{9,... | collective-permute-start | bytes 307208 | tf_op jit(solution)/shard_map/ppermute | solution.py:42
  53.4 2.2 %collective-permute-start.15 = (bf16[40,1280]{1,0:T(8,128)(2,1)S(1)}, bf16[40,1280]{1,0:T(8,128)(2,1)S(1)}, u32[]{:S(2)}, u32[]{:S(2)}) collective-permute-start(bf16[40,1280]{1,0:T(8,128)(2,1)S(1)} %shard_map.64.refs_4_.refs_0_), channel_id=1, source_target_pairs={{0,24},{1,25},{2,26},{3,27},{4,28},{5,29},{6,30},{7,31},{8,0},{9,1... | collective-permute-start | bytes 307208 | tf_op jit(solution)/shard_map/ppermute | solution.py:42
  55.7 3.0 %collective-permute-start.18 = (bf16[40,1280]{1,0:T(8,128)(2,1)S(1)}, bf16[40,1280]{1,0:T(8,128)(2,1)S(1)}, u32[]{:S(2)}, u32[]{:S(2)}) collective-permute-start(bf16[40,1280]{1,0:T(8,128)(2,1)S(1)} %shard_map.65.refs_4_), channel_id=1, source_target_pairs={{0,64},{1,65},{2,66},{3,67},{4,68},{5,69},{6,70},{7,71},{8,72},{9,... | collective-permute-start | bytes 307208 | tf_op jit(solution)/shard_map/ppermute | solution.py:42
  59.4 1.3 %collective-permute-start.20 = (bf16[40,1280]{1,0:T(8,128)(2,1)S(1)}, bf16[40,1280]{1,0:T(8,128)(2,1)S(1)}, u32[]{:S(2)}, u32[]{:S(2)}) collective-permute-start(bf16[40,1280]{1,0:T(8,128)(2,1)S(1)} %shard_map.65.refs_4_), channel_id=1, source_target_pairs={{0,32},{1,33},{2,34},{3,35},{4,36},{5,37},{6,38},{7,39},{8,40},{9,... | collective-permute-start | bytes 307208 | tf_op jit(solution)/shard_map/ppermute | solution.py:42
  61.9 1.4 %collective-permute-done.19.refs_6_ = bf16[40,1280]{1,0:T(8,128)(2,1)S(1)} collective-permute-done((bf16[40,1280]{1,0:T(8,128)(2,1)S(1)}, bf16[40,1280]{1,0:T(8,128)(2,1)S(1)}, u32[]{:S(2)}, u32[]{:S(2)}) %collective-permute-start.19) | collective-permute-done | bytes 102432 | tf_op jit(solution)/shard_map/ppermute | solution.py:42
  63.3 1.9 %collective-permute-done.20.refs_7_ = bf16[40,1280]{1,0:T(8,128)(2,1)S(1)} collective-permute-done((bf16[40,1280]{1,0:T(8,128)(2,1)S(1)}, bf16[40,1280]{1,0:T(8,128)(2,1)S(1)}, u32[]{:S(2)}, u32[]{:S(2)}) %collective-permute-start.20) | collective-permute-done | bytes 102432 | tf_op jit(solution)/shard_map/ppermute | solution.py:42
  65.3 1.7 %collective-permute-start.25 = (bf16[4,40,1280]{2,1,0:T(8,128)(2,1)S(1)}, bf16[4,40,1280]{2,1,0:T(8,128)(2,1)S(1)}, u32[]{:S(2)}, u32[]{:S(2)}) collective-permute-start(bf16[4,40,1280]{2,1,0:T(8,128)(2,1)S(1)} %get-tuple-element.32.refs_0_.refs_6_), channel_id=1, source_target_pairs={{0,16},{1,17},{2,18},{3,19},{4,20},{5,21},{6,22},{7,23},{8,24},{9,... | collective-permute-start | bytes 1228808 | tf_op jit(solution)/shard_map/ppermute | solution.py:42
  67.0 2.6 %collective-permute-start.26 = (bf16[4,40,1280]{2,1,0:T(8,128)(2,1)S(1)}, bf16[4,40,1280]{2,1,0:T(8,128)(2,1)S(1)}, u32[]{:S(2)}, u32[]{:S(2)}) collective-permute-start(bf16[4,40,1280]{2,1,0:T(8,128)(2,1)S(1)} %get-tuple-element.32.refs_0_.refs_6_), channel_id=1, source_target_pairs={{0,24},{1,25},{2,26},{3,27},{4,28},{5,29},{6,30},{7,31},{8,0},{9,1... | collective-permute-start | bytes 1228808 | tf_op jit(solution)/shard_map/ppermute | solution.py:42
  70.1 2.1 %collective-permute-start.24 = (bf16[4,40,1280]{2,1,0:T(8,128)(2,1)S(1)}, bf16[4,40,1280]{2,1,0:T(8,128)(2,1)S(1)}, u32[]{:S(2)}, u32[]{:S(2)}) collective-permute-start(bf16[4,40,1280]{2,1,0:T(8,128)(2,1)S(1)} %get-tuple-element.31.refs_0_), channel_id=1, source_target_pairs={{0,96},{1,97},{2,98},{3,99},{4,100},{5,101},{6,102},{7,103},{8,104... | collective-permute-start | bytes 1228808 | tf_op jit(solution)/shard_map/ppermute | solution.py:42
  72.3 7.1 %collective-permute-done.25.refs_1_ = bf16[4,40,1280]{2,1,0:T(8,128)(2,1)S(1)} collective-permute-done((bf16[4,40,1280]{2,1,0:T(8,128)(2,1)S(1)}, bf16[4,40,1280]{2,1,0:T(8,128)(2,1)S(1)}, u32[]{:S(2)}, u32[]{:S(2)}) %collective-permute-start.25) | collective-permute-done | bytes 409632 | tf_op jit(solution)/shard_map/ppermute | solution.py:42
  80.3 4.2 %collective-permute-done.26.refs_2_ = bf16[4,40,1280]{2,1,0:T(8,128)(2,1)S(1)} collective-permute-done((bf16[4,40,1280]{2,1,0:T(8,128)(2,1)S(1)}, bf16[4,40,1280]{2,1,0:T(8,128)(2,1)S(1)}, u32[]{:S(2)}, u32[]{:S(2)}) %collective-permute-start.26) | collective-permute-done | bytes 409632 | tf_op jit(solution)/shard_map/ppermute | solution.py:42
  84.6 1.3 %shard_map.68.refs_3_ = bf16[8,80,2560]{2,1,0:T(8,128)(2,1)} custom-call(bf16[4,40,1280]{2,1,0:T(8,128)(2,1)S(1)} %get-tuple-element.32.refs_0_.refs_6_, bf16[4,40,1280]{2,1,0:T(8,128)(2,1)S(1)} %collective-permute-done.25.refs_1_, bf16[4,40,1280]{2,1,0:T(8,128)(2,1)S(1)} %collective-permute-done.26.refs_2_, ...), custom_call_target="tpu_custom_call" | custom-call | flops 4915200 | bytes 4915200 | tf_op jit(solution)/shard_map/pallas_call | solution.py:66
  85.9 1.0 %collective-permute-done.24.refs_2_ = bf16[4,40,1280]{2,1,0:T(8,128)(2,1)S(1)} collective-permute-done((bf16[4,40,1280]{2,1,0:T(8,128)(2,1)S(1)}, bf16[4,40,1280]{2,1,0:T(8,128)(2,1)S(1)}, u32[]{:S(2)}, u32[]{:S(2)}) %collective-permute-start.24) | collective-permute-done | bytes 409632 | tf_op jit(solution)/shard_map/ppermute | solution.py:42
  86.9 1.2 %shard_map.69.refs_1_ = bf16[8,80,2560]{2,1,0:T(8,128)(2,1)} custom-call(bf16[4,40,1280]{2,1,0:T(8,128)(2,1)S(1)} %get-tuple-element.31.refs_0_, bf16[4,40,1280]{2,1,0:T(8,128)(2,1)S(1)} %collective-permute-done.23.refs_1_, bf16[4,40,1280]{2,1,0:T(8,128)(2,1)S(1)} %collective-permute-done.24.refs_2_, ...), custom_call_target="tpu_custom_call", output_to_operand_aliasing={{}: (3, {})} | custom-call | flops 7782400 | bytes 7782400 | tf_op jit(solution)/shard_map/pallas_call | solution.py:66
  (46 shorter events, 7.6 us)
Async XLA Ops:
  0.6 7.0 %copy-start.2 = (bf16[1,640,2560]{2,1,0:T(8,128)(2,1)S(1)}, bf16[1,640,2560]{2,1,0:T(8,128)(2,1)}, u32[]{:S(2)}) copy-start(bf16[1,640,2560]{2,1,0:T(8,128)(2,1)} %param.3) | copy-start | bytes 9830404
  2.3 14.1 %copy-start = (f32[20,2560]{1,0:T(8,128)S(1)}, f32[20,2560]{1,0:T(8,128)}, u32[]{:S(2)}) copy-start(f32[20,2560]{1,0:T(8,128)} %refs_5_.1) | copy-start | bytes 614404
  2.3 14.1 %copy-start.1 = (f32[20,2560]{1,0:T(8,128)S(1)}, f32[20,2560]{1,0:T(8,128)}, u32[]{:S(2)}) copy-start(f32[20,2560]{1,0:T(8,128)} %refs_0_.1) | copy-start | bytes 614404
  2.3 12.6 %collective-permute-start = (bf16[80,2560]{1,0:T(8,128)(2,1)S(1)}, bf16[80,2560]{1,0:T(8,128)(2,1)S(1)}, u32[]{:S(2)}, u32[]{:S(2)}) collective-permute-start(bf16[80,2560]{1,0:T(8,128)(2,1)S(1)} %get-tuple-element.37), channel_id=1, source_target_pairs={{0,32},{1,33},{2,34},{3,35},{4,36},{5,37},{6,38},{7,39},{8,40},{9,... | collective-permute-start | bytes 1228808 | tf_op jit(solution)/shard_map/ppermute | solution.py:42
  4.0 19.1 %collective-permute-start.1 = (bf16[80,2560]{1,0:T(8,128)(2,1)S(1)}, bf16[80,2560]{1,0:T(8,128)(2,1)S(1)}, u32[]{:S(2)}, u32[]{:S(2)}) collective-permute-start(bf16[80,2560]{1,0:T(8,128)(2,1)S(1)} %get-tuple-element.36), channel_id=1, source_target_pairs={{0,96},{1,97},{2,98},{3,99},{4,100},{5,101},{6,102},{7,103},{8,104... | collective-permute-start | bytes 1228808 | tf_op jit(solution)/shard_map/ppermute | solution.py:42
  5.7 23.7 %collective-permute-start.2 = (bf16[80,2560]{1,0:T(8,128)(2,1)S(1)}, bf16[80,2560]{1,0:T(8,128)(2,1)S(1)}, u32[]{:S(2)}, u32[]{:S(2)}) collective-permute-start(bf16[80,2560]{1,0:T(8,128)(2,1)S(1)} %get-tuple-element.35), channel_id=1, source_target_pairs={{0,64},{1,65},{2,66},{3,67},{4,68},{5,69},{6,70},{7,71},{8,72},{9,... | collective-permute-start | bytes 1228808 | tf_op jit(solution)/shard_map/ppermute | solution.py:42
  8.0 23.3 %collective-permute-start.6 = (bf16[80,2560]{1,0:T(8,128)(2,1)S(1)}, bf16[80,2560]{1,0:T(8,128)(2,1)S(1)}, u32[]{:S(2)}, u32[]{:S(2)}) collective-permute-start(bf16[80,2560]{1,0:T(8,128)(2,1)S(1)} %get-tuple-element.24), channel_id=1, source_target_pairs={{0,16},{1,17},{2,18},{3,19},{4,20},{5,21},{6,22},{7,23},{8,24},{9,... | collective-permute-start | bytes 1228808 | tf_op jit(solution)/shard_map/ppermute | solution.py:42
  11.1 22.0 %collective-permute-start.7 = (bf16[80,2560]{1,0:T(8,128)(2,1)S(1)}, bf16[80,2560]{1,0:T(8,128)(2,1)S(1)}, u32[]{:S(2)}, u32[]{:S(2)}) collective-permute-start(bf16[80,2560]{1,0:T(8,128)(2,1)S(1)} %get-tuple-element.25), channel_id=1, source_target_pairs={{0,24},{1,25},{2,26},{3,27},{4,28},{5,29},{6,30},{7,31},{8,0},{9,1... | collective-permute-start | bytes 1228808 | tf_op jit(solution)/shard_map/ppermute | solution.py:42
  14.9 20.0 %collective-permute-start.8 = (bf16[80,2560]{1,0:T(8,128)(2,1)S(1)}, bf16[80,2560]{1,0:T(8,128)(2,1)S(1)}, u32[]{:S(2)}, u32[]{:S(2)}) collective-permute-start(bf16[80,2560]{1,0:T(8,128)(2,1)S(1)} %get-tuple-element.26), channel_id=1, source_target_pairs={{0,8},{1,9},{2,10},{3,11},{4,12},{5,13},{6,14},{7,15},{8,16},{9,17... | collective-permute-start | bytes 1228808 | tf_op jit(solution)/shard_map/ppermute | solution.py:42
  23.1 18.3 %collective-permute-start.9 = (f32[20,2560]{1,0:T(8,128)S(1)}, f32[20,2560]{1,0:T(8,128)S(1)}, u32[]{:S(2)}, u32[]{:S(2)}) collective-permute-start(f32[20,2560]{1,0:T(8,128)S(1)} %shard_map.61.refs_2_.refs_4_), channel_id=1, source_target_pairs={{0,128},{1,129},{2,130},{3,131},{4,132},{5,133},{6,134},{7,135},{8... | collective-permute-start | bytes 614408 | tf_op jit(solution)/shard_map/ppermute | solution.py:42
  29.8 5.9 %collective-permute-start.3 = (bf16[40,1280]{1,0:T(8,128)(2,1)S(1)}, bf16[40,1280]{1,0:T(8,128)(2,1)S(1)}, u32[]{:S(2)}, u32[]{:S(2)}) collective-permute-start(bf16[40,1280]{1,0:T(8,128)(2,1)S(1)} %get-tuple-element.20), channel_id=1, source_target_pairs={{0,8},{1,9},{2,10},{3,11},{4,12},{5,13},{6,14},{7,15},{8,16},{9,17... | collective-permute-start | bytes 307208 | tf_op jit(solution)/shard_map/ppermute | solution.py:42
  31.3 8.0 %collective-permute-start.4 = (bf16[40,1280]{1,0:T(8,128)(2,1)S(1)}, bf16[40,1280]{1,0:T(8,128)(2,1)S(1)}, u32[]{:S(2)}, u32[]{:S(2)}) collective-permute-start(bf16[40,1280]{1,0:T(8,128)(2,1)S(1)} %get-tuple-element.21), channel_id=1, source_target_pairs={{0,24},{1,25},{2,26},{3,27},{4,28},{5,29},{6,30},{7,31},{8,0},{9,1... | collective-permute-start | bytes 307208 | tf_op jit(solution)/shard_map/ppermute | solution.py:42
  33.1 8.2 %collective-permute-start.5 = (bf16[40,1280]{1,0:T(8,128)(2,1)S(1)}, bf16[40,1280]{1,0:T(8,128)(2,1)S(1)}, u32[]{:S(2)}, u32[]{:S(2)}) collective-permute-start(bf16[40,1280]{1,0:T(8,128)(2,1)S(1)} %get-tuple-element.22), channel_id=1, source_target_pairs={{0,16},{1,17},{2,18},{3,19},{4,20},{5,21},{6,22},{7,23},{8,24},{9,... | collective-permute-start | bytes 307208 | tf_op jit(solution)/shard_map/ppermute | solution.py:42
  35.3 9.5 %collective-permute-start.11 = (bf16[40,1280]{1,0:T(8,128)(2,1)S(1)}, bf16[40,1280]{1,0:T(8,128)(2,1)S(1)}, u32[]{:S(2)}, u32[]{:S(2)}) collective-permute-start(bf16[40,1280]{1,0:T(8,128)(2,1)S(1)} %get-tuple-element.28), channel_id=1, source_target_pairs={{0,32},{1,33},{2,34},{3,35},{4,36},{5,37},{6,38},{7,39},{8,40},{9,... | collective-permute-start | bytes 307208 | tf_op jit(solution)/shard_map/ppermute | solution.py:42
  35.7 9.1 %collective-permute-start.12 = (bf16[40,1280]{1,0:T(8,128)(2,1)S(1)}, bf16[40,1280]{1,0:T(8,128)(2,1)S(1)}, u32[]{:S(2)}, u32[]{:S(2)}) collective-permute-start(bf16[40,1280]{1,0:T(8,128)(2,1)S(1)} %get-tuple-element.29), channel_id=1, source_target_pairs={{0,96},{1,97},{2,98},{3,99},{4,100},{5,101},{6,102},{7,103},{8,104... | collective-permute-start | bytes 307208 | tf_op jit(solution)/shard_map/ppermute | solution.py:42
  39.4 6.2 %collective-permute-start.13 = (bf16[40,1280]{1,0:T(8,128)(2,1)S(1)}, bf16[40,1280]{1,0:T(8,128)(2,1)S(1)}, u32[]{:S(2)}, u32[]{:S(2)}) collective-permute-start(bf16[40,1280]{1,0:T(8,128)(2,1)S(1)} %get-tuple-element.30), channel_id=1, source_target_pairs={{0,64},{1,65},{2,66},{3,67},{4,68},{5,69},{6,70},{7,71},{8,72},{9,... | collective-permute-start | bytes 307208 | tf_op jit(solution)/shard_map/ppermute | solution.py:42
  41.4 9.5 %collective-permute-start.10 = (bf16[40,1280]{1,0:T(8,128)(2,1)S(1)}, bf16[40,1280]{1,0:T(8,128)(2,1)S(1)}, u32[]{:S(2)}, u32[]{:S(2)}) collective-permute-start(bf16[40,1280]{1,0:T(8,128)(2,1)S(1)} %shard_map.62.refs_4_.refs_0_), channel_id=1, source_target_pairs={{0,128},{1,129},{2,130},{3,131},{4,132},{5,133},{6,134},{7,135},{8... | collective-permute-start | bytes 307208 | tf_op jit(solution)/shard_map/ppermute | solution.py:42
  45.6 10.0 %collective-permute-start.17 = (bf16[40,1280]{1,0:T(8,128)(2,1)S(1)}, bf16[40,1280]{1,0:T(8,128)(2,1)S(1)}, u32[]{:S(2)}, u32[]{:S(2)}) collective-permute-start(bf16[40,1280]{1,0:T(8,128)(2,1)S(1)} %shard_map.63.refs_4_.refs_0_.refs_2_), channel_id=1, source_target_pairs={{0,128},{1,129},{2,130},{3,131},{4,132},{5,133},{6,134},{7,135},{8... | collective-permute-start | bytes 307208 | tf_op jit(solution)/shard_map/ppermute | solution.py:42
  50.9 8.4 %collective-permute-start.14 = (bf16[40,1280]{1,0:T(8,128)(2,1)S(1)}, bf16[40,1280]{1,0:T(8,128)(2,1)S(1)}, u32[]{:S(2)}, u32[]{:S(2)}) collective-permute-start(bf16[40,1280]{1,0:T(8,128)(2,1)S(1)} %shard_map.64.refs_4_.refs_0_), channel_id=1, source_target_pairs={{0,16},{1,17},{2,18},{3,19},{4,20},{5,21},{6,22},{7,23},{8,24},{9,... | collective-permute-start | bytes 307208 | tf_op jit(solution)/shard_map/ppermute | solution.py:42
  53.4 7.3 %collective-permute-start.15 = (bf16[40,1280]{1,0:T(8,128)(2,1)S(1)}, bf16[40,1280]{1,0:T(8,128)(2,1)S(1)}, u32[]{:S(2)}, u32[]{:S(2)}) collective-permute-start(bf16[40,1280]{1,0:T(8,128)(2,1)S(1)} %shard_map.64.refs_4_.refs_0_), channel_id=1, source_target_pairs={{0,24},{1,25},{2,26},{3,27},{4,28},{5,29},{6,30},{7,31},{8,0},{9,1... | collective-permute-start | bytes 307208 | tf_op jit(solution)/shard_map/ppermute | solution.py:42
  55.6 5.9 %collective-permute-start.16 = (bf16[40,1280]{1,0:T(8,128)(2,1)S(1)}, bf16[40,1280]{1,0:T(8,128)(2,1)S(1)}, u32[]{:S(2)}, u32[]{:S(2)}) collective-permute-start(bf16[40,1280]{1,0:T(8,128)(2,1)S(1)} %shard_map.64.refs_4_.refs_0_), channel_id=1, source_target_pairs={{0,8},{1,9},{2,10},{3,11},{4,12},{5,13},{6,14},{7,15},{8,16},{9,17... | collective-permute-start | bytes 307208 | tf_op jit(solution)/shard_map/ppermute | solution.py:42
  55.7 6.3 %collective-permute-start.18 = (bf16[40,1280]{1,0:T(8,128)(2,1)S(1)}, bf16[40,1280]{1,0:T(8,128)(2,1)S(1)}, u32[]{:S(2)}, u32[]{:S(2)}) collective-permute-start(bf16[40,1280]{1,0:T(8,128)(2,1)S(1)} %shard_map.65.refs_4_), channel_id=1, source_target_pairs={{0,64},{1,65},{2,66},{3,67},{4,68},{5,69},{6,70},{7,71},{8,72},{9,... | collective-permute-start | bytes 307208 | tf_op jit(solution)/shard_map/ppermute | solution.py:42
  58.6 4.7 %collective-permute-start.19 = (bf16[40,1280]{1,0:T(8,128)(2,1)S(1)}, bf16[40,1280]{1,0:T(8,128)(2,1)S(1)}, u32[]{:S(2)}, u32[]{:S(2)}) collective-permute-start(bf16[40,1280]{1,0:T(8,128)(2,1)S(1)} %shard_map.65.refs_4_), channel_id=1, source_target_pairs={{0,96},{1,97},{2,98},{3,99},{4,100},{5,101},{6,102},{7,103},{8,104... | collective-permute-start | bytes 307208 | tf_op jit(solution)/shard_map/ppermute | solution.py:42
  59.4 5.9 %collective-permute-start.20 = (bf16[40,1280]{1,0:T(8,128)(2,1)S(1)}, bf16[40,1280]{1,0:T(8,128)(2,1)S(1)}, u32[]{:S(2)}, u32[]{:S(2)}) collective-permute-start(bf16[40,1280]{1,0:T(8,128)(2,1)S(1)} %shard_map.65.refs_4_), channel_id=1, source_target_pairs={{0,32},{1,33},{2,34},{3,35},{4,36},{5,37},{6,38},{7,39},{8,40},{9,... | collective-permute-start | bytes 307208 | tf_op jit(solution)/shard_map/ppermute | solution.py:42
  61.5 3.8 %collective-permute-start.21 = (f32[8,128]{1,0:T(8,128)S(1)}, f32[8,128]{1,0:T(8,128)S(1)}, u32[]{:S(2)}, u32[]{:S(2)}) collective-permute-start(f32[8,128]{1,0:T(8,128)S(1)} %shard_map.66), channel_id=1, source_target_pairs={{0,1},{1,0},{2,3},{3,2},{4,5},{5,4},{6,7},{7,6},{8,9},{9,8},{10,11... | collective-permute-start | bytes 12296 | tf_op jit(solution)/shard_map/ppermute | solution.py:42
  65.3 14.0 %collective-permute-start.25 = (bf16[4,40,1280]{2,1,0:T(8,128)(2,1)S(1)}, bf16[4,40,1280]{2,1,0:T(8,128)(2,1)S(1)}, u32[]{:S(2)}, u32[]{:S(2)}) collective-permute-start(bf16[4,40,1280]{2,1,0:T(8,128)(2,1)S(1)} %get-tuple-element.32.refs_0_.refs_6_), channel_id=1, source_target_pairs={{0,16},{1,17},{2,18},{3,19},{4,20},{5,21},{6,22},{7,23},{8,24},{9,... | collective-permute-start | bytes 1228808 | tf_op jit(solution)/shard_map/ppermute | solution.py:42
  67.0 17.5 %collective-permute-start.26 = (bf16[4,40,1280]{2,1,0:T(8,128)(2,1)S(1)}, bf16[4,40,1280]{2,1,0:T(8,128)(2,1)S(1)}, u32[]{:S(2)}, u32[]{:S(2)}) collective-permute-start(bf16[4,40,1280]{2,1,0:T(8,128)(2,1)S(1)} %get-tuple-element.32.refs_0_.refs_6_), channel_id=1, source_target_pairs={{0,24},{1,25},{2,26},{3,27},{4,28},{5,29},{6,30},{7,31},{8,0},{9,1... | collective-permute-start | bytes 1228808 | tf_op jit(solution)/shard_map/ppermute | solution.py:42
  69.7 14.9 %collective-permute-start.27 = (bf16[4,40,1280]{2,1,0:T(8,128)(2,1)S(1)}, bf16[4,40,1280]{2,1,0:T(8,128)(2,1)S(1)}, u32[]{:S(2)}, u32[]{:S(2)}) collective-permute-start(bf16[4,40,1280]{2,1,0:T(8,128)(2,1)S(1)} %get-tuple-element.32.refs_0_.refs_6_), channel_id=1, source_target_pairs={{0,8},{1,9},{2,10},{3,11},{4,12},{5,13},{6,14},{7,15},{8,16},{9,17... | collective-permute-start | bytes 1228808 | tf_op jit(solution)/shard_map/ppermute | solution.py:42
  69.7 16.2 %collective-permute-start.23 = (bf16[4,40,1280]{2,1,0:T(8,128)(2,1)S(1)}, bf16[4,40,1280]{2,1,0:T(8,128)(2,1)S(1)}, u32[]{:S(2)}, u32[]{:S(2)}) collective-permute-start(bf16[4,40,1280]{2,1,0:T(8,128)(2,1)S(1)} %get-tuple-element.31.refs_0_), channel_id=1, source_target_pairs={{0,64},{1,65},{2,66},{3,67},{4,68},{5,69},{6,70},{7,71},{8,72},{9,... | collective-permute-start | bytes 1228808 | tf_op jit(solution)/shard_map/ppermute | solution.py:42
  70.1 16.8 %collective-permute-start.24 = (bf16[4,40,1280]{2,1,0:T(8,128)(2,1)S(1)}, bf16[4,40,1280]{2,1,0:T(8,128)(2,1)S(1)}, u32[]{:S(2)}, u32[]{:S(2)}) collective-permute-start(bf16[4,40,1280]{2,1,0:T(8,128)(2,1)S(1)} %get-tuple-element.31.refs_0_), channel_id=1, source_target_pairs={{0,96},{1,97},{2,98},{3,99},{4,100},{5,101},{6,102},{7,103},{8,104... | collective-permute-start | bytes 1228808 | tf_op jit(solution)/shard_map/ppermute | solution.py:42
  79.4 9.2 %collective-permute-start.22 = (bf16[4,40,1280]{2,1,0:T(8,128)(2,1)S(1)}, bf16[4,40,1280]{2,1,0:T(8,128)(2,1)S(1)}, u32[]{:S(2)}, u32[]{:S(2)}) collective-permute-start(bf16[4,40,1280]{2,1,0:T(8,128)(2,1)S(1)} %get-tuple-element.31.refs_0_), channel_id=1, source_target_pairs={{0,32},{1,33},{2,34},{3,35},{4,36},{5,37},{6,38},{7,39},{8,40},{9,... | collective-permute-start | bytes 1228808 | tf_op jit(solution)/shard_map/ppermute | solution.py:42
